TPU v7x, 128 devices: a whole 4x4x4 slice. The times are simulated.
128 devices in a mesh: row: 8 (over y, x_hi), col: 16 (over z, x_lo, core).
Axes of the slice: x: 4 (x_hi: 2, x_lo: 2; x = x_hi * 2 + x_lo), y: 4, z: 4, core: 2. Of those that a mesh axis runs over, the one named last changes fastest.
Arguments:
- teacher: bfloat16 [16384, 256], replicated, may hold values from -4 to 4
- panel_ids: int32 [2048], P('col'), may hold values from 0 to 16383
- rest_ids: int32 [8, 16, 128], P('row', 'col'), may hold values from 0 to 16383
- inverse: bfloat16 [2048, 2048], replicated, may hold values from -1 to 1, as said below
Outputs:
- trailing: float32 [16, 8, 128, 8, 16, 128], P(None, 'row', None, None, 'col')
- panel_rows: bfloat16 [8, 16, 128, 2048], P('row', 'col')
Inputs may be any that keep to these rules, and one draw needn't show every extreme that they name: `inverse`: zero above the diagonal.
All inputs are finite; a program needn't handle non-finite values.
Results may differ from a plain program's by a relative error of at most 0.0049.
Values may be sent and summed in bfloat16 or wider, within the bound.
No kernel may reach another device: no remote copies, remote signals or barrier semaphores. Data moves between devices by JAX's collectives and lax.ppermute only.
A program may use at most 128 MiB of HBM per device.

v0:
```python
import jax
import jax.numpy as jnp
from jax import lax
from jax.sharding import PartitionSpec as P


def gaussian(left_rows, right_rows, inv_scale):
    sq_left = jnp.sum(jnp.square(left_rows.astype(jnp.float32)), axis=-1)
    sq_right = jnp.sum(jnp.square(right_rows.astype(jnp.float32)), axis=-1)
    inner = lax.dot_general(
        left_rows, right_rows, (((1,), (1,)), ((), ())), preferred_element_type=jnp.float32
    )
    return jnp.exp(-inv_scale * (sq_left[:, None] + sq_right[None, :] - 2.0 * inner))


def factor(rows_emb, panel_emb, inverse, inv_scale):
    kernel = gaussian(rows_emb, panel_emb, inv_scale).astype(jnp.bfloat16)
    block_width = inverse.shape[0] // 4
    pieces = []
    for block_at in range(4):
        finish = (block_at + 1) * block_width
        pieces.append(
            lax.dot_general(
                kernel[:, :finish],
                inverse[block_at * block_width : finish, :finish],
                (((1,), (1,)), ((), ())),
                preferred_element_type=jnp.float32,
            )
        )
    return jnp.concatenate(pieces, 1).astype(jnp.bfloat16)


def shards(teacher, panel_ids, rest_ids, inverse):
    n_row = lax.axis_size("row")
    n_col = lax.axis_size("col")
    row_at = lax.axis_index("row")
    col_at = lax.axis_index("col")
    stretch_rows = rest_ids.shape[2]
    inv_scale = 2.0 / teacher.shape[1]
    gathered = lax.all_gather(rest_ids, ("row", "col"), axis=0, tiled=True)
    blocks = gathered.reshape(n_row * n_col, stretch_rows)
    panel = lax.all_gather(panel_ids, "col", axis=0, tiled=True)
    panel_emb = teacher[panel]
    own_ids = lax.dynamic_slice_in_dim(blocks, row_at * n_col + col_at, 1, 0).reshape(stretch_rows)
    col_ids = lax.dynamic_slice_in_dim(
        blocks.reshape(n_row, n_col, stretch_rows), col_at, 1, 1
    ).reshape(-1)
    row_ids = lax.dynamic_slice_in_dim(
        blocks.reshape(n_col, n_row, stretch_rows), row_at, 1, 1
    ).reshape(-1)
    own_factor = factor(teacher[own_ids], panel_emb, inverse, inv_scale)
    col_emb = teacher[col_ids]
    col_factor = lax.all_gather(own_factor, "row", axis=0, tiled=True)
    row_emb = teacher[row_ids]
    kernel = gaussian(row_emb, col_emb, inv_scale)
    local_ids = lax.dynamic_slice_in_dim(blocks, col_at * n_row + row_at, 1, 0).reshape(
        stretch_rows
    )
    local_factor = factor(teacher[local_ids], panel_emb, inverse, inv_scale)
    update = lax.dot_general(
        lax.all_gather(local_factor, "col", axis=0, tiled=True),
        col_factor,
        (((1,), (1,)), ((), ())),
        preferred_element_type=jnp.float32,
    )
    rows_local = jnp.arange(n_col * stretch_rows, dtype=jnp.int32)
    row_index = (
        rows_local // stretch_rows * n_row + row_at
    ) * stretch_rows + rows_local % stretch_rows
    cols_local = jnp.arange(n_row * stretch_rows, dtype=jnp.int32)
    col_index = (
        cols_local // stretch_rows * n_col + col_at
    ) * stretch_rows + cols_local % stretch_rows
    result = kernel - update
    trailing = jnp.where(row_index[:, None] >= col_index[None, :], result, jnp.zeros_like(result))
    return (
        trailing.reshape(n_col, 1, stretch_rows, n_row, 1, stretch_rows),
        own_factor.reshape(1, 1, stretch_rows, own_factor.shape[1]),
    )


def solution(mesh):
    return jax.shard_map(
        shards,
        mesh=mesh,
        in_specs=(P(), P("col"), P("row", "col", None), P()),
        out_specs=(P(None, "row", None, None, "col", None), P("row", "col", None, None)),
        check_vma=False,
    )
```

profile of v0, /device:TPU:1, one launch (start us, length us, event | category | flops | bytes accessed | tf_op | source)
XLA Modules:
  0.0 375.2 jit_solution(5608160516560032385)
XLA Ops:
  7.2 0.0 all-gather.6.cloned.1.call-start
  7.2 179.5 %all_gather.12 = s32[128,1,128]{2,1,0:T(1,128)S(1)} all-gather(s32[1,1,128]{2,1,0:T(1,128)} %param.6), channel_id=1, replica_groups=mesh['row'=8,'col'=16] {'row','col'}, dimensions={0}, use_global_device_ids=true | all-gather | bytes 66048 | tf_op jit(solution)/shard_map/all_gather | solution.py:40
  186.8 5.2 %gather_fusion.4 = bf16[128,256]{1,0:T(8,128)(2,1)S(1)} fusion(bf16[16384,256]{1,0:T(8,128)(2,1)} %param.4, s32[1024]{0:T(1024)S(1)} %get-tuple-element.8), kind=kCustom, calls=%fused_computation.4 | custom fusion | bytes 131584 | tf_op jit(solution)/shard_map/gather | solution.py:51
  192.0 0.1 multiply_reduce_fusion.3
  192.1 16.3 %all-gather = s32[16,1,128]{2,1,0:T(1,128)S(1)} all-gather(s32[1,1,128]{2,1,0:T(1,128)} %bitcast.57), channel_id=1, replica_groups=mesh['row'=8,'col'=16] {'col'}, dimensions={0}, use_global_device_ids=true | all-gather | bytes 8704 | tf_op jit(solution)/shard_map/all_gather | solution.py:42
  208.4 11.1 %gather_fusion.3 = bf16[2048,256]{1,0:T(8,128)(2,1)S(1)} fusion(bf16[16384,256]{1,0:T(8,128)(2,1)} %param.4, s32[2048]{0:T(1024)S(1)} %fusion.49), kind=kCustom, calls=%fused_computation.3 | custom fusion | bytes 2105344 | tf_op jit(solution)/shard_map/gather | solution.py:43
  219.5 0.3 multiply_reduce_fusion
  219.9 0.5 fusion.7
  220.4 1.4 convolution_convert_fusion
  221.7 1.7 convolution_convert_fusion.2
  223.5 2.4 fusion.19
  225.9 2.1 fusion.25
  228.0 0.9 pad_maximum_fusion.1
  228.8 0.0 all-gather.6.cloned.1.call-update
  228.9 0.0 all-gather.4.cloned.1.call-start
  228.9 5.2 %gather_fusion.2 = bf16[128,256]{1,0:T(8,128)(2,1)S(1)} fusion(bf16[16384,256]{1,0:T(8,128)(2,1)} %param.4, s32[1024]{0:T(1024)S(1)} %get-tuple-element.9), kind=kCustom, calls=%fused_computation.2 | custom fusion | bytes 131584 | tf_op jit(solution)/shard_map/gather | solution.py:59
  234.1 0.1 multiply_reduce_fusion.4
  234.2 0.5 fusion.6
  234.8 1.4 convolution_convert_fusion.1
  236.1 1.7 convolution_convert_fusion.3
  237.9 2.1 fusion.22
  239.9 2.4 fusion.16
  242.4 0.8 pad_maximum_fusion
  243.2 0.0 all-gather.4.cloned.1.call-update
  243.3 11.3 %gather_fusion = bf16[2048,256]{1,0:T(8,128)(2,1)S(1)} fusion(bf16[16384,256]{1,0:T(8,128)(2,1)} %param.4, s32[2048]{0:T(1024)S(1)} %broadcast_clamp_fusion), kind=kCustom, calls=%fused_computation | custom fusion | bytes 2105344 | tf_op jit(solution)/shard_map/gather | solution.py:54
  254.7 7.9 %gather_fusion.1 = bf16[1024,256]{1,0:T(8,128)(2,1)S(1)} fusion(bf16[16384,256]{1,0:T(8,128)(2,1)} %param.4, s32[1024]{0:T(1024)S(1)} %broadcast_clamp_fusion.1), kind=kCustom, calls=%fused_computation.1 | custom fusion | bytes 1052672 | tf_op jit(solution)/shard_map/gather | solution.py:52
  262.6 0.2 multiply_reduce_fusion.2
  262.8 0.3 multiply_reduce_fusion.1
  263.2 0.8 pad_maximum_fusion.2
  264.0 30.3 %all-gather.6.cloned.1.call-done = bf16[1024,2048]{1,0:T(8,128)(2,1)} async-done(((bf16[128,2048]{1,0:T(8,128)(2,1)}), bf16[1024,2048]{1,0:T(8,128)(2,1)}) %all-gather.6.cloned.1.call-update) | async-done | bytes 4194320 | tf_op jit(solution)/shard_map/all_gather | solution.py:53
  294.4 53.2 %all-gather.4.cloned.1.call-done = bf16[2048,2048]{1,0:T(8,128)(2,1)} async-done(((bf16[128,2048]{1,0:T(8,128)(2,1)}), bf16[2048,2048]{1,0:T(8,128)(2,1)}) %all-gather.4.cloned.1.call-update) | async-done | bytes 8388624 | tf_op jit(solution)/shard_map/all_gather | solution.py:61
  347.6 12.5 %fusion.65 = f32[2048,1024]{1,0:T(8,128)S(1)} fusion(bf16[2048,2048]{1,0:T(8,128)(2,1)} %all-gather.4.cloned.1.call-done, bf16[1024,2048]{1,0:T(8,128)(2,1)} %all-gather.6.cloned.1.call-done), kind=kOutput, calls=%fused_computation.96 | convolution fusion | flops 8589934592 | bytes 20971520 | tf_op jit(solution)/shard_map/dot_general | solution.py:60
  360.1 2.8 select_bitcast_fusion
  362.9 5.5 %copy.8 = f32[256,8,8,128]{3,2,1,0:T(8,128)} copy(f32[256,8,8,128]{3,1,2,0:T(8,128)S(1)} %select_bitcast_fusion) | data formatting | bytes 16777216
  (9 shorter events, 0.1 us)
Async XLA Ops:
  7.2 287.2 %all-gather.6.cloned.1.call-start = ((), (), s32[]{:S(2)}) async-start(), calls=%async_computation.1 | async-start | bytes 4718592 | tf_op jit(solution)/shard_map/all_gather | solution.py:53
  228.9 118.7 %all-gather.4.cloned.1.call-start = ((), (), s32[]{:S(2)}) async-start(), calls=%async_computation | async-start | bytes 8912896 | tf_op jit(solution)/shard_map/all_gather | solution.py:61
Sparse Core Ops, SparseCore 0:
  229.0 65.3 all-gather.5
  296.6 50.8 all-gather.3
where the time goes:
time: 376 us; the launch traced here: 375 us
  blocking collectives  196 us (52%)
  waiting for transfers between devices  83.6 us (22%)
  local copies, waits for them, and re-layouts  46.3 us (12%)
  matrix products  31.4 us (8%)
  between operations  14.2 us (4%)
  other arithmetic  3.77 us (1%)
    all_gather x1, blocking collectives, shards(): gathered = lax.all_gather(rest_ids, ('row', 'col'), axis=0, tiled=True)  180 us
    all_gather x1, waiting for transfers between devices, shards(): lax.all_gather(local_factor, 'col', axis=0, tiled=True)  53.2 us
    all_gather x1, waiting for transfers between devices, shards(): col_factor = lax.all_gather(own_factor, 'row', axis=0, tiled=True)  30.3 us
    all_gather x1, blocking collectives, shards(): panel = lax.all_gather(panel_ids, 'col', axis=0, tiled=True)  16.3 us
    dot_general x8, matrix products, factor(): lax.dot_general(kernel[:, :finish], inverse[block_at * block_width:finish...  15.1 us
    dot_general x1, matrix products, shards(): lax.dot_general(lax.all_gather(local_factor, 'col', axis=0, tiled=True),...  12.5 us
    gather x1, local copies, waits for them, and re-layouts, shards(): row_emb = teacher[row_ids]  11.3 us
    gather x1, local copies, waits for them, and re-layouts, shards(): panel_emb = teacher[panel]  11.1 us
  transfers between devices with their start and end apart: 2, of which 2 were waited for; matrix products, arithmetic and copies ran while one was open for 9% of the time, Pallas kernels for 0%

commit v1 on v0

v1 whole, which is shorter than its diff:
```python
import jax
import jax.numpy as jnp
from jax import lax
from jax.sharding import PartitionSpec as P


def sq_norms(rows):
    return jnp.sum(jnp.square(rows.astype(jnp.float32)), axis=-1)


def gaussian(left_rows, right_rows, inv_scale):
    inner = lax.dot_general(
        left_rows, right_rows, (((1,), (1,)), ((), ())), preferred_element_type=jnp.float32
    )
    return jnp.exp(
        -inv_scale * (sq_norms(left_rows)[:, None] + sq_norms(right_rows)[None, :] - 2.0 * inner)
    )


def factor(kernel, inverse):
    n_blocks = 4
    block_width = inverse.shape[0] // n_blocks
    pieces = []
    for block_at in range(n_blocks):
        finish = (block_at + 1) * block_width
        pieces.append(
            lax.dot_general(
                kernel[:, :finish],
                inverse[block_at * block_width : finish, :finish],
                (((1,), (1,)), ((), ())),
                preferred_element_type=jnp.float32,
            ).astype(jnp.bfloat16)
        )
    return jnp.concatenate(pieces, 1)


def shards(teacher, panel_ids, rest_ids, inverse):
    n_row = lax.axis_size("row")
    n_col = lax.axis_size("col")
    row_at = lax.axis_index("row")
    col_at = lax.axis_index("col")
    stretch_rows = rest_ids.shape[2]
    inv_scale = 2.0 / teacher.shape[1]
    both = jnp.concatenate([rest_ids.reshape(1, -1), panel_ids.reshape(1, -1)], 0)
    both = jnp.broadcast_to(both[None], (n_row * n_col, *both.shape))
    both = lax.all_to_all(both, ("row", "col"), 0, 0, tiled=True)
    panel = both[:n_col, 1].reshape(-1)
    blocks = both[:, 0]
    col_ids = lax.dynamic_index_in_dim(
        blocks.reshape(n_row, n_col, stretch_rows), col_at, 1, False
    ).reshape(-1)
    row_ids = lax.dynamic_index_in_dim(
        blocks.reshape(n_col, n_row, stretch_rows), row_at, 1, False
    ).reshape(-1)
    n_col_ids, n_row_ids = col_ids.shape[0], row_ids.shape[0]
    emb = teacher[jnp.concatenate([col_ids, row_ids, panel])]
    x_emb = emb[: n_col_ids + n_row_ids]
    panel_emb = emb[n_col_ids + n_row_ids :]
    col_emb, row_emb = x_emb[:n_col_ids], x_emb[n_col_ids:]
    cross = gaussian(x_emb, panel_emb, inv_scale).astype(jnp.bfloat16)
    factors = factor(cross, inverse)
    col_factor, row_factor = factors[:n_col_ids], factors[n_col_ids:]
    own_factor = lax.dynamic_slice_in_dim(col_factor, row_at * stretch_rows, stretch_rows, 0)
    update = lax.dot_general(
        row_factor, col_factor, (((1,), (1,)), ((), ())), preferred_element_type=jnp.float32
    )
    rows_local = jnp.arange(n_col * stretch_rows, dtype=jnp.int32)
    row_index = (
        rows_local // stretch_rows * n_row + row_at
    ) * stretch_rows + rows_local % stretch_rows
    cols_local = jnp.arange(n_row * stretch_rows, dtype=jnp.int32)
    col_index = (
        cols_local // stretch_rows * n_col + col_at
    ) * stretch_rows + cols_local % stretch_rows
    result = gaussian(row_emb, col_emb, inv_scale) - update
    trailing = jnp.where(row_index[:, None] >= col_index[None, :], result, jnp.zeros_like(result))
    return (
        trailing.reshape(n_col, 1, stretch_rows, n_row, 1, stretch_rows),
        own_factor.reshape(1, 1, stretch_rows, own_factor.shape[1]),
    )


def solution(mesh):
    return jax.shard_map(
        shards,
        mesh=mesh,
        in_specs=(P(), P("col"), P("row", "col", None), P()),
        out_specs=(P(None, "row", None, None, "col", None), P("row", "col", None, None)),
        check_vma=False,
    )
```

time: 376 us -> 122 us (0.32)
  blocking collectives: 196 us -> 0 us
  waiting for transfers between devices: 83.6 us -> 10.2 us
  matrix products: 31.4 us -> 57 us
  local copies, waits for them, and re-layouts: 46.3 us -> 29 us
  between operations: 14.2 us -> 0.79 us
  starting transfers between devices: 0.08 us -> 11.5 us
  other arithmetic: 3.77 us -> 13 us
    all_gather x2 -> x0, blocking collectives: 196 us -> none  [the longest x1 180 us: shards(): gathered = lax.all_gather(rest_ids, ('row', 'col'), axis=0, tiled=True)]
    all_gather x2 -> x0, waiting for transfers between devices: 83.5 us -> none  [the longest x1 53.2 us: shards(): lax.all_gather(local_factor, 'col', axis=0, tiled=True)]
    gather x5 -> x1, local copies, waits for them, and re-layouts: 40.8 us -> 20.6 us  [shards(): emb = teacher[jnp.concatenate([col_ids, row_ids, panel])]]
    dot_general x8 -> x4, matrix products: 15.1 us -> 29.4 us  [factor(): lax.dot_general(kernel[:, :finish], inverse[block_at * block_width:finish...]
    all_to_all x0 -> x1, starting transfers between devices: none -> 11.5 us  [shards(): both = lax.all_to_all(both, ('row', 'col'), 0, 0, tiled=True)]
    dot_general x3 -> x2, matrix products: 3.79 us -> 14.4 us  [gaussian(): lax.dot_general(left_rows, right_rows, (((1,), (1,)), ((), ())), preferre...]
    all_to_all x0 -> x1, waiting for transfers between devices: none -> 10.2 us  [shards(): both = lax.all_to_all(both, ('row', 'col'), 0, 0, tiled=True)]
    slice x0 -> x1, other arithmetic: none -> 9.43 us  [shards(): col_factor, row_factor = (factors[:n_col_ids], factors[n_col_ids:])]
  transfers between devices with their start and end apart: 2 -> 1, of which waited for: 2 -> 1; matrix products, arithmetic and copies ran while one was open for 9% -> 0% of each run, Pallas kernels for 0% -> 0%
where the time goes in v1:
time: 122 us; the launch traced here: 121 us
  matrix products  57 us (47%)
  local copies, waits for them, and re-layouts  29 us (24%)
  other arithmetic  13 us (11%)
  starting transfers between devices  11.5 us (9%)
  waiting for transfers between devices  10.2 us (8%)
    dot_general x4, matrix products, factor(): lax.dot_general(kernel[:, :finish], inverse[block_at * block_width:finish...  29.4 us
    gather x1, local copies, waits for them, and re-layouts, shards(): emb = teacher[jnp.concatenate([col_ids, row_ids, panel])]  20.6 us
    dot_general x2, matrix products, gaussian(): lax.dot_general(left_rows, right_rows, (((1,), (1,)), ((), ())), preferre...  14.4 us
    dot_general x1, matrix products, shards(): lax.dot_general(row_factor, col_factor, (((1,), (1,)), ((), ())), preferr...  13.3 us
    all_to_all x1, starting transfers between devices, shards(): both = lax.all_to_all(both, ('row', 'col'), 0, 0, tiled=True)  11.5 us
    all_to_all x1, waiting for transfers between devices, shards(): both = lax.all_to_all(both, ('row', 'col'), 0, 0, tiled=True)  10.2 us
    slice x1, other arithmetic, shards(): col_factor, row_factor = (factors[:n_col_ids], factors[n_col_ids:])  9.43 us
    unnamed x5, local copies, waits for them, and re-layouts  5.49 us
  transfers between devices with their start and end apart: 1, of which 1 were waited for; matrix products, arithmetic and copies ran while one was open for 0% of the time, Pallas kernels for 0%

profile of v1, /device:TPU:1, one launch (start us, length us, event | category | flops | bytes accessed | tf_op | source)
XLA Modules:
  0.0 121.4 jit_solution(13103693943620825869)
XLA Ops:
  0.6 0.7 pad_add_fusion
  1.3 0.7 broadcast_in_dim.4
  2.0 11.5 %all-to-all-start = ((s32[128,2,128]{2,1,0:T(2,128)}), s32[128,2,128]{2,1,0:T(2,128)S(1)}, u32[]{:S(2)}, u32[]{:S(2)}) async-start(s32[128,2,128]{2,1,0:T(2,128)} %broadcast_in_dim.4), calls=%async_computation | async-start | bytes 262144 | tf_op jit(solution)/shard_map/all_to_all | solution.py:46
  13.5 10.2 %all-to-all-done = s32[128,2,128]{2,1,0:T(2,128)S(1)} async-done(((s32[128,2,128]{2,1,0:T(2,128)}), s32[128,2,128]{2,1,0:T(2,128)S(1)}, u32[]{:S(2)}, u32[]{:S(2)}) %all-to-all-start) | async-done | bytes 131104 | tf_op jit(solution)/shard_map/all_to_all | solution.py:46
  23.8 20.6 %gather_fusion = bf16[5120,256]{1,0:T(8,128)(2,1)S(1)} fusion(bf16[16384,256]{1,0:T(8,128)(2,1)} %param.4, s32[5120]{0:T(1024)S(1)} %broadcast_clamp_fusion), kind=kCustom, calls=%fused_computation | custom fusion | bytes 5263360 | tf_op jit(solution)/shard_map/gather | solution.py:56
  44.5 0.6 multiply_reduce_fusion.2
  45.1 0.0 slice-start
  45.1 0.5 multiply_reduce_fusion
  45.6 0.0 slice-start.1
  45.6 8.2 %exponential_convert_fusion = bf16[3072,2048]{1,0:T(8,128)(2,1)} fusion(f32[2048]{0:T(1024)S(1)} %get-tuple-element.7, f32[3072]{0:T(1024)S(1)} %multiply_reduce_fusion, bf16[5120,256]{1,0:T(8,128)(2,1)S(1)} %gather_fusion), kind=kOutput, calls=%fused_computation.1 | convolution fusion | flops 3252682752 | bytes 15224832 | tf_op jit(solution)/shard_map/dot_general | solution.py:12
  53.8 0.0 slice-done
  53.8 0.0 slice-done.1
  53.8 9.9 %convolution_convert_fusion = bf16[3072,512]{0,1:T(8,128)(2,1)S(1)} fusion(bf16[3072,2048]{1,0:T(8,128)(2,1)} %exponential_convert_fusion, bf16[2048,2048]{1,0:T(8,128)(2,1)S(1)} %bitcast.29), kind=kOutput, calls=%fused_computation.12 | convolution fusion | flops 6444023808 | bytes 17825792 | tf_op jit(solution)/shard_map/dot_general | solution.py:27
  63.7 3.7 %convolution_convert_fusion.1 = bf16[3072,512]{0,1:T(8,128)(2,1)S(1)} fusion(bf16[3072,2048]{1,0:T(8,128)(2,1)} %exponential_convert_fusion, bf16[2048,2048]{1,0:T(8,128)(2,1)S(1)} %bitcast.29), kind=kOutput, calls=%fused_computation.13 | convolution fusion | flops 1612185600 | bytes 6815744 | tf_op jit(solution)/shard_map/dot_general | solution.py:27
  67.5 6.6 %fusion.6 = bf16[3072,512]{0,1:T(8,128)(2,1)S(1)} fusion(bf16[3072,2048]{1,0:T(8,128)(2,1)} %exponential_convert_fusion, bf16[2048,2048]{1,0:T(8,128)(2,1)S(1)} %bitcast.29), kind=kOutput, calls=%fused_computation.10 | convolution fusion | flops 3222798336 | bytes 10485760 | tf_op jit(solution)/shard_map/dot_general | solution.py:27
  74.1 9.2 %fusion.9 = bf16[3072,512]{0,1:T(8,128)(2,1)S(1)} fusion(bf16[3072,2048]{1,0:T(8,128)(2,1)} %exponential_convert_fusion, bf16[2048,2048]{1,0:T(8,128)(2,1)S(1)} %bitcast.29), kind=kOutput, calls=%fused_computation.11 | convolution fusion | flops 4833411072 | bytes 14155776 | tf_op jit(solution)/shard_map/dot_general | solution.py:27
  83.2 1.5 %pad_maximum_fusion = bf16[3072,2048]{0,1:T(8,128)(2,1)S(1)} fusion(bf16[3072,512]{0,1:T(8,128)(2,1)S(1)} %convolution_convert_fusion, bf16[3072,512]{0,1:T(8,128)(2,1)S(1)} %fusion.9, bf16[3072,512]{0,1:T(8,128)(2,1)S(1)} %fusion.6, bf16[3072,512]{0,1:T(8,128)(2,1)S(1)} %convolution_convert_fusion.1), kind=kLoop, calls=%fused_computation.2 | loop fusion | flops 50331648 | bytes 25165824 | tf_op jit(solution)/shard_map/concatenate | solution.py:34
  84.8 9.4 %pad_maximum_fusion.1 = bf16[1024,2048]{0,1:T(8,128)(2,1)} fusion(bf16[3072,512]{0,1:T(8,128)(2,1)S(1)} %convolution_convert_fusion, bf16[3072,512]{0,1:T(8,128)(2,1)S(1)} %fusion.9, bf16[3072,512]{0,1:T(8,128)(2,1)S(1)} %fusion.6, bf16[3072,512]{0,1:T(8,128)(2,1)S(1)} %convolution_convert_fusion.1), kind=kLoop, calls=%fused_computation.14 | loop fusion | flops 16777216 | bytes 16777216 | tf_op jit(solution)/shard_map/slice | solution.py:62
  94.2 0.2 multiply_reduce_fusion.3
  94.4 13.3 %fusion.2 = f32[2048,1024]{1,0:T(8,128)} fusion(bf16[1024,2048]{0,1:T(8,128)(2,1)} %pad_maximum_fusion.1, bf16[3072,2048]{0,1:T(8,128)(2,1)S(1)} %pad_maximum_fusion), kind=kOutput, calls=%fused_computation.5 | convolution fusion | flops 8589934592 | bytes 20971520 | tf_op jit(solution)/shard_map/dot_general | solution.py:64
  107.7 6.2 %select_bitcast_fusion = f32[256,8,8,128]{3,1,2,0:T(8,128)S(1)} fusion(f32[2048,1024]{1,0:T(8,128)} %fusion.2, f32[1024]{0:T(1024)S(1)} %multiply_reduce_fusion.3, f32[2048]{0:T(1024)S(1)} %get-tuple-element.6, s32[1024]{0:T(1024)S(1)} %fusion.41, s32[2048]{0:T(1024)S(1)} %fusion.30, bf16[5120,256]{1,0:T(8,128)(2,1)S(1)} %gather_fusion), kind=kOutput, calls=%fused_computation.7 | convolution fusion | flops 1088421888 | bytes 18374656 | tf_op jit(solution)/shard_map/dot_general | solution.py:12
  113.9 5.5 %copy.9 = f32[256,8,8,128]{3,2,1,0:T(8,128)} copy(f32[256,8,8,128]{3,1,2,0:T(8,128)S(1)} %select_bitcast_fusion) | data formatting | bytes 16777216
  119.3 1.1 constant_dynamic-slice_fusion
  120.4 1.0 copy.7
  (8 shorter events, 0.1 us)
Async XLA Ops:
  2.0 21.7 %all-to-all-start = ((s32[128,2,128]{2,1,0:T(2,128)}), s32[128,2,128]{2,1,0:T(2,128)S(1)}, u32[]{:S(2)}, u32[]{:S(2)}) async-start(s32[128,2,128]{2,1,0:T(2,128)} %broadcast_in_dim.4), calls=%async_computation | async-start | bytes 262144 | tf_op jit(solution)/shard_map/all_to_all | solution.py:46
  45.1 8.7 %slice-start = ((s8[8388608]{0:T(1024)(128)(4,1)}), s8[4194304]{0:T(1024)(128)(4,1)S(1)}, s32[]{:S(2)}) async-start(s8[8388608]{0:T(1024)(128)(4,1)} %bitcast.28), calls=%async_computation.1 | async-start | bytes 8388608
  45.6 8.2 %slice-start.1 = ((s8[8388608]{0:T(1024)(128)(4,1)}), s8[4194304]{0:T(1024)(128)(4,1)S(1)}, s32[]{:S(2)}) async-start(s8[8388608]{0:T(1024)(128)(4,1)} %bitcast.28), calls=%async_computation.2 | async-start | bytes 8388608

commit v2 on v1

v2 whole, which is shorter than its diff:
```python
import functools
import math

import jax
import jax.numpy as jnp
from jax import lax
from jax.experimental import pallas as pl
from jax.experimental.pallas import tpu as pltpu
from jax.sharding import PartitionSpec as P

BF16, F32 = jnp.bfloat16, jnp.float32
MIB = 1 << 20
LANES = 128
CHUNK = 512
WIDE = 256


def nt_dot(left, right):
    return lax.dot_general(left, right, (((1,), (1,)), ((), ())), preferred_element_type=F32)


def column_norms(rows, scale):
    wide = rows.astype(F32)
    return scale * jnp.sum(wide * wide, axis=1, keepdims=True)


def lane_norms(rows, scale):
    wide = rows.astype(F32)
    square = wide * wide
    high = square.astype(BF16)
    low = (square - high.astype(F32)).astype(BF16)
    ones = jnp.ones((8, rows.shape[1]), BF16)
    return scale * (nt_dot(ones, high) + nt_dot(ones, low))


def split_kernel(scale, n_sets, teacher_ref, panel_ids, row_ids, col_ids, inverse_ref,
                 factor_out, panel_out, norm_out, row_out, col_out,
                 left, right, stage_left, stage_right, cross, ids, sems):
    row_at, col_at = lax.axis_index("row"), lax.axis_index("col")
    n_panel, n_rows, n_cols = n_sets
    copies = [
        pltpu.make_async_copy(panel_ids.at[pl.ds(0, n_panel), 1], ids.at[pl.ds(0, n_panel)], sems.at[0]),
        pltpu.make_async_copy(row_ids.at[:, row_at, 0], ids.at[pl.ds(n_panel, n_rows)], sems.at[1]),
        pltpu.make_async_copy(col_ids.at[:, col_at, 0], ids.at[pl.ds(n_panel + n_rows, n_cols)], sems.at[2]),
    ]
    for copy in copies:
        copy.start()

    def widen(step, carry):
        at = pl.ds(pl.multiple_of(step * CHUNK, CHUNK), CHUNK)
        left[at, :] = teacher_ref[at, :LANES].astype(F32)
        right[at, :] = teacher_ref[at, LANES:].astype(F32)
        return carry

    lax.fori_loop(0, teacher_ref.shape[0] // CHUNK, widen, 0)
    for copy in copies:
        copy.wait()

    stretch = ids.shape[2]

    def gather(first_block, out):
        def chunk(step, carry):
            def some(part, carry):
                for u in range(32):
                    at = part * 32 + u
                    row = ids[first_block + step * (CHUNK // stretch) + part // (stretch // 32), 0,
                              (part % (stretch // 32)) * 32 + u]
                    stage_left[pl.ds(at, 1), :] = left[pl.ds(row, 1), :]
                    stage_right[pl.ds(at, 1), :] = right[pl.ds(row, 1), :]
                return carry

            lax.fori_loop(0, CHUNK // 32, some, 0)
            to = pl.ds(pl.multiple_of(step * CHUNK, CHUNK), CHUNK)
            out[to, :LANES] = stage_left[...].astype(BF16)
            out[to, LANES:] = stage_right[...].astype(BF16)
            return carry

        lax.fori_loop(0, out.shape[0] // CHUNK, chunk, 0)

    gather(0, panel_out)
    for at in range(0, panel_out.shape[0], CHUNK):
        norm_out[:, at : at + CHUNK] = lane_norms(panel_out[at : at + CHUNK, :], scale)
    gather(n_panel, row_out)
    half = factor_out.shape[0]
    mine = pl.multiple_of(col_at % 2 * half, half)
    factor_rows(scale, row_out[pl.ds(mine, half), :], panel_out, norm_out, inverse_ref, cross, factor_out)
    gather(n_panel + n_rows, col_out)


def factor_rows(scale, rows, panel_ref, norm_ref, inverse_ref, cross, factor_ref):
    norms = column_norms(rows, scale)
    for at in range(0, panel_ref.shape[0], WIDE):
        to = slice(at, at + WIDE)
        inner = nt_dot(rows, panel_ref[to, :])
        cross[:, to] = jnp.exp2(2.0 * scale * inner - norms - norm_ref[:1, to]).astype(BF16)
        factor_ref[:, to] = nt_dot(cross[:, : at + WIDE], inverse_ref[to, : at + WIDE]).astype(BF16)


def column_kernel(scale, stretch, col_ref, panel_ref, norm_ref, inverse_ref, factor_out, own_out, cross, sem):
    factor_rows(scale, col_ref[...], panel_ref, norm_ref, inverse_ref, cross, factor_out)
    own = pl.ds(pl.multiple_of(lax.axis_index("row") * stretch, stretch), stretch)
    copy = pltpu.make_async_copy(factor_out.at[own], own_out, sem)
    copy.start()
    copy.wait()


def update_kernel(scale, n_row, n_col, stretch, mine_hbm, other_hbm, factor_ref, row_ref, col_ref, out_hbm,
                  rows, stage, norms, in_sems, out_sems):
    row_at, col_at = lax.axis_index("row"), lax.axis_index("col")
    tile = rows.shape[1]
    n_tiles = row_ref.shape[0] // tile
    half_tiles = mine_hbm.shape[0] // tile
    parity = col_at % 2
    for at in range(0, col_ref.shape[0], CHUNK):
        norms[:, at : at + CHUNK] = lane_norms(col_ref[at : at + CHUNK, :], scale)

    def fetch(m, slot):
        src = pl.ds(pl.multiple_of(m % half_tiles * tile, tile), tile)

        @pl.when(m // half_tiles == parity)
        def _():
            pltpu.make_async_copy(mine_hbm.at[src], rows.at[slot], in_sems.at[slot]).start()

        @pl.when(m // half_tiles != parity)
        def _():
            pltpu.make_async_copy(other_hbm.at[src], rows.at[slot], in_sems.at[slot]).start()

    def put(m, slot):
        size = stage.shape[1]
        return pltpu.make_async_copy(
            stage.at[slot], out_hbm.at[pl.ds(pl.multiple_of(m * size, size), size)], out_sems.at[slot])

    fetch(n_tiles - 1, 0)
    above = lax.broadcasted_iota(jnp.int32, (tile, LANES), 0)
    above = above // stretch * (n_row * stretch) + above % stretch - lax.broadcasted_iota(jnp.int32, (tile, LANES), 1)

    def one_tile(step, carry):
        m = n_tiles - 1 - step
        slot = step % 2

        @pl.when(step + 1 < n_tiles)
        def _():
            fetch(m - 1, 1 - slot)

        @pl.when(step >= 2)
        def _():
            put(m + 2, slot).wait()

        pltpu.make_async_copy(mine_hbm.at[pl.ds(0, tile)], rows.at[slot], in_sems.at[slot]).wait()
        rows_emb = row_ref[pl.ds(pl.multiple_of(m * tile, tile), tile), :]
        row_norms = column_norms(rows_emb, scale)
        first_row = (m * (tile // stretch) * n_row + row_at) * stretch

        for n in range(factor_ref.shape[0] // WIDE):
            blocks = [(n * (WIDE // LANES) + b) for b in range(WIDE // LANES)]

            @pl.when(n <= m)
            def _():
                to = slice(n * WIDE, (n + 1) * WIDE)
                update = nt_dot(rows[slot], factor_ref[to, :])
                inner = nt_dot(rows_emb, col_ref[to, :])
                result = jnp.exp2(2.0 * scale * inner - row_norms - norms[:1, to]) - update
                for b, block in enumerate(blocks):
                    first_col = (block * n_col + col_at) * stretch
                    piece = result[:, b * LANES : (b + 1) * LANES]
                    piece = jnp.where(above >= first_col - first_row, piece, 0.0)
                    stage[slot, pl.ds(block, tile, stride=n_row), :] = piece

            @pl.when(n > m)
            def _():
                for block in blocks:
                    stage[slot, pl.ds(block, tile, stride=n_row), :] = jnp.zeros((tile, LANES), F32)

        put(m, slot).start()
        return carry

    lax.fori_loop(0, n_tiles, one_tile, 0)
    put(1, (n_tiles - 2) % 2).wait()
    put(0, (n_tiles - 1) % 2).wait()


def shards(teacher, panel_ids, rest_ids, inverse):
    n_row, n_col = lax.axis_size("row"), lax.axis_size("col")
    stretch = rest_ids.shape[2]
    width = inverse.shape[0]
    n_rows, n_cols = n_col * stretch, n_row * stretch
    half = n_rows // 2
    scale = 2.0 / teacher.shape[1] * math.log2(math.e)
    vmem = pl.BlockSpec(memory_space=pltpu.VMEM)
    hbm = pl.BlockSpec(memory_space=pl.ANY)
    both = jnp.concatenate([rest_ids.reshape(1, 1, -1), panel_ids.reshape(1, 1, -1)], 0)
    both = jnp.broadcast_to(both[None], (n_row * n_col, *both.shape))
    both = lax.all_to_all(both, ("row", "col"), 0, 0, tiled=True)

    mine, panel_emb, panel_norms, row_emb, col_emb = pl.pallas_call(
        functools.partial(split_kernel, scale, (n_col, n_col, n_row)),
        out_shape=(
            jax.ShapeDtypeStruct((half, width), BF16),
            jax.ShapeDtypeStruct((width, teacher.shape[1]), BF16),
            jax.ShapeDtypeStruct((8, width), F32),
            jax.ShapeDtypeStruct((n_rows, teacher.shape[1]), BF16),
            jax.ShapeDtypeStruct((n_cols, teacher.shape[1]), BF16),
        ),
        in_specs=[vmem, hbm, hbm, hbm, vmem],
        out_specs=[vmem] * 5,
        scratch_shapes=[
            pltpu.VMEM((teacher.shape[0], LANES), F32),
            pltpu.VMEM((teacher.shape[0], LANES), F32),
            pltpu.VMEM((CHUNK, LANES), F32),
            pltpu.VMEM((CHUNK, LANES), F32),
            pltpu.VMEM((half, width), BF16),
            pltpu.SMEM((2 * n_col + n_row, 1, stretch), jnp.int32),
            pltpu.SemaphoreType.DMA((3,)),
        ],
        compiler_params=pltpu.CompilerParams(vmem_limit_bytes=56 * MIB),
        name="rows",
    )(teacher, both, both.reshape(n_col, n_row, 2, 1, stretch), both.reshape(n_row, n_col, 2, 1, stretch), inverse)

    other = lax.ppermute(mine, "col", [(i, i ^ 1) for i in range(n_col)])

    factors, own = pl.pallas_call(
        functools.partial(column_kernel, scale, stretch),
        out_shape=(
            jax.ShapeDtypeStruct((n_cols, width), BF16),
            jax.ShapeDtypeStruct((stretch, width), BF16),
        ),
        in_specs=[vmem] * 4,
        out_specs=[vmem, hbm],
        scratch_shapes=[pltpu.VMEM((n_cols, width), BF16), pltpu.SemaphoreType.DMA],
        compiler_params=pltpu.CompilerParams(vmem_limit_bytes=32 * MIB),
        cost_estimate=pl.CostEstimate(
            flops=2 * n_cols * width * width, bytes_accessed=16 * MIB, transcendentals=n_cols * width),
        name="columns",
    )(col_emb, panel_emb, panel_norms, inverse)

    tile = 4 * stretch
    trailing = pl.pallas_call(
        functools.partial(update_kernel, scale, n_row, n_col, stretch),
        out_shape=jax.ShapeDtypeStruct((n_rows * n_row, stretch), F32),
        in_specs=[hbm, hbm, vmem, vmem, vmem],
        out_specs=hbm,
        scratch_shapes=[
            pltpu.VMEM((2, tile, width), BF16),
            pltpu.VMEM((2, tile * n_row, stretch), F32),
            pltpu.VMEM((8, n_cols), F32),
            pltpu.SemaphoreType.DMA((2,)),
            pltpu.SemaphoreType.DMA((2,)),
        ],
        compiler_params=pltpu.CompilerParams(vmem_limit_bytes=32 * MIB),
        name="update",
    )(mine, other, factors, row_emb, col_emb)
    return (
        trailing.reshape(n_col, 1, stretch, n_row, 1, stretch),
        own.reshape(1, 1, stretch, width),
    )


def solution(mesh):
    return jax.shard_map(
        shards,
        mesh=mesh,
        in_specs=(P(), P("col"), P("row", "col", None), P()),
        out_specs=(P(None, "row", None, None, "col", None), P("row", "col", None, None)),
        check_vma=False,
    )
```

time: 122 us -> 82.9 us (0.68)
  matrix products: 57 us -> 0 us
  Pallas kernels: 0 us -> 52 us
  local copies, waits for them, and re-layouts: 29 us -> 6.56 us
  blocking collectives: 0 us -> 21.9 us
  other arithmetic: 13 us -> 0.67 us
  starting transfers between devices: 11.5 us -> 0.66 us
  waiting for transfers between devices: 10.2 us -> 0.01 us
    dot_general x7 -> x0, matrix products: 57 us -> none  [the longest x4 29.4 us: factor(): lax.dot_general(kernel[:, :finish], inverse[block_at * block_width:finish...]
    pallas_call x0 -> x3, Pallas kernels: none -> 52 us  [the longest x1 31.8 us: shards(): pl.pallas_call(functools.partial(split_kernel, scale, (n_col, n_col, n_ro...]
    all_to_all x0 -> x1, blocking collectives: none -> 21.9 us  [shards(): both = lax.all_to_all(both, ('row', 'col'), 0, 0, tiled=True)]
    gather x1 -> x0, local copies, waits for them, and re-layouts: 20.6 us -> none  [shards(): emb = teacher[jnp.concatenate([col_ids, row_ids, panel])]]
    all_to_all x1 -> x0, starting transfers between devices: 11.5 us -> none  [shards(): both = lax.all_to_all(both, ('row', 'col'), 0, 0, tiled=True)]
    all_to_all x1 -> x0, waiting for transfers between devices: 10.2 us -> none  [shards(): both = lax.all_to_all(both, ('row', 'col'), 0, 0, tiled=True)]
    slice x1 -> x0, other arithmetic: 9.43 us -> none  [shards(): col_factor, row_factor = (factors[:n_col_ids], factors[n_col_ids:])]
    dynamic_slice x2 -> x0, local copies, waits for them, and re-layouts: 2.08 us -> none  [shards(): lax.dynamic_slice_in_dim(col_factor, row_at * stretch_rows, stretch_rows, 0)]
  transfers between devices with their start and end apart: 1 -> 1, of which waited for: 1 -> 0; matrix products, arithmetic and copies ran while one was open for 0% -> 0% of each run, Pallas kernels for 0% -> 9%
where the time goes in v2:
time: 82.9 us; the launch traced here: 82.6 us
  Pallas kernels  52 us (63%)
  blocking collectives  21.9 us (26%)
  local copies, waits for them, and re-layouts  6.56 us (8%)
  between operations  0.84 us (1%)
    pallas_call x1, Pallas kernels, shards(): pl.pallas_call(functools.partial(split_kernel, scale, (n_col, n_col, n_ro...  31.8 us
    all_to_all x1, blocking collectives, shards(): both = lax.all_to_all(both, ('row', 'col'), 0, 0, tiled=True)  21.9 us
    pallas_call x1, Pallas kernels, shards(): pl.pallas_call(functools.partial(update_kernel, scale, n_row, n_col, stre...  12.4 us
    pallas_call x1, Pallas kernels, shards(): pl.pallas_call(functools.partial(column_kernel, scale, stretch), out_shap...  7.77 us
    unnamed x12, local copies, waits for them, and re-layouts  6.49 us
  transfers between devices with their start and end apart: 1, of which 0 were waited for; matrix products, arithmetic and copies ran while one was open for 0% of the time, Pallas kernels for 9%

profile of v2, /device:TPU:1, one launch (start us, length us, event | category | flops | bytes accessed | tf_op | source)
XLA Modules:
  0.0 82.6 jit_solution(7103160202935704179)
XLA Ops:
  0.6 0.7 pad_add_fusion
  1.3 0.1 broadcast_in_dim.9
  1.4 21.9 %all_to_all.5.panel_ids = s32[128,2,1,128]{3,2,1,0:T(1,128)} all-to-all(s32[128,2,1,128]{3,2,1,0:T(1,128)S(1)} %broadcast_in_dim.9), channel_id=1, replica_groups=mesh['row'=8,'col'=16] {'row','col'}, dimensions={0} | all-to-all | bytes 262144 | tf_op jit(solution)/shard_map/all_to_all | solution.py:193
  23.2 31.8 %rows.1 = (bf16[1024,2048]{1,0:T(8,128)(2,1)}, bf16[2048,256]{1,0:T(8,128)(2,1)}, f32[8,2048]{1,0:T(8,128)}, bf16[2048,256]{1,0:T(8,128)(2,1)}, bf16[1024,256]{1,0:T(8,128)(2,1)}) custom-call(bf16[16384,256]{1,0:T(8,128)(2,1)} %teacher_ref.1, s32[128,2,1,128]{3,2,1,0:T(1,128)} %all_to_all.5.panel_ids, s32[16,8,2,1,128]{4,3,2,1,0:T(1,128)} %bitcast.9, ...), custom_call_target="tpu_custom_call" | custom-call | tf_op jit(solution)/shard_map/rows/pallas_call | solution.py:195
  55.1 0.7 collective-permute-start
  55.7 0.0 copy-start
  55.7 3.4 %copy-done = bf16[2048,2048]{1,0:T(8,128)(2,1)S(1)} copy-done((bf16[2048,2048]{1,0:T(8,128)(2,1)S(1)}, bf16[2048,2048]{1,0:T(8,128)(2,1)}, u32[]{:S(2)}) %copy-start) | copy-done | bytes 8388632
  59.1 0.0 copy-start.3
  59.1 1.0 %copy-done.3 = bf16[1024,256]{1,0:T(8,128)(2,1)S(1)} copy-done((bf16[1024,256]{1,0:T(8,128)(2,1)S(1)}, bf16[1024,256]{1,0:T(8,128)(2,1)}, u32[]{:S(2)}) %copy-start.3) | copy-done | bytes 524312
  60.2 0.0 copy-start.4
  60.2 1.2 %copy-done.4 = bf16[2048,256]{1,0:T(8,128)(2,1)S(1)} copy-done((bf16[2048,256]{1,0:T(8,128)(2,1)S(1)}, bf16[2048,256]{1,0:T(8,128)(2,1)}, u32[]{:S(2)}) %copy-start.4) | copy-done | bytes 1048600
  61.4 0.0 copy-start.5
  61.4 0.8 %copy-done.5 = f32[8,2048]{1,0:T(8,128)S(1)} copy-done((f32[8,2048]{1,0:T(8,128)S(1)}, f32[8,2048]{1,0:T(8,128)}, u32[]{:S(2)}) %copy-start.5) | copy-done | bytes 65560
  62.2 0.0 copy-start.1
  62.2 0.0 copy-start.2
  62.2 7.8 %columns.1 = (bf16[1024,2048]{1,0:T(8,128)(2,1)S(1)}, bf16[128,2048]{1,0:T(8,128)(2,1)}) custom-call(bf16[1024,256]{1,0:T(8,128)(2,1)S(1)} %copy-done.3, bf16[2048,256]{1,0:T(8,128)(2,1)S(1)} %copy-done.4, f32[8,2048]{1,0:T(8,128)S(1)} %copy-done.5, bf16[2048,2048]{1,0:T(8,128)(2,1)S(1)} %copy-done), custom_call_target="tpu_custom_call" | custom-call | flops 8589934592 | bytes 16777216 | tf_op jit(solution)/shard_map/columns/pallas_call | solution.py:221
  70.0 0.0 collective-permute-done.other_hbm
  70.0 0.0 copy-done.1
  70.0 0.0 copy-done.2
  70.0 12.4 %update.1 = f32[16384,128]{1,0:T(8,128)} custom-call(bf16[1024,2048]{1,0:T(8,128)(2,1)S(1)} %copy-done.1, bf16[1024,2048]{1,0:T(8,128)(2,1)S(1)} %collective-permute-done.other_hbm, bf16[1024,2048]{1,0:T(8,128)(2,1)S(1)} %get-tuple-element.13.factor_ref, bf16[2048,256]{1,0:T(8,128)(2,1)S(1)} %copy-done.2, bf16[1024,256]{1,0:T(8,128)(2,1)S(1)} %copy-done.3), custom_call_target="tpu_custom_call" | custom-call | tf_op jit(solution)/shard_map/update/pallas_call | solution.py:237
Async XLA Ops:
  55.1 14.9 %collective-permute-start = (bf16[1024,2048]{1,0:T(8,128)(2,1)}, bf16[1024,2048]{1,0:T(8,128)(2,1)S(1)}, u32[]{:S(2)}, u32[]{:S(2)}) collective-permute-start(bf16[1024,2048]{1,0:T(8,128)(2,1)} %get-tuple-element.9.mine_hbm), channel_id=1, source_target_pairs={{0,1},{1,0},{2,3},{3,2},{4,5},{5,4},{6,7},{7,6},{8,9},{9,8},{10,11... | collective-permute-start | bytes 12582920 | tf_op jit(solution)/shard_map/ppermute | solution.py:219
  55.7 3.4 %copy-start = (bf16[2048,2048]{1,0:T(8,128)(2,1)S(1)}, bf16[2048,2048]{1,0:T(8,128)(2,1)}, u32[]{:S(2)}) copy-start(bf16[2048,2048]{1,0:T(8,128)(2,1)} %inverse_ref.3) | copy-start | bytes 25165828
  59.1 1.0 %copy-start.3 = (bf16[1024,256]{1,0:T(8,128)(2,1)S(1)}, bf16[1024,256]{1,0:T(8,128)(2,1)}, u32[]{:S(2)}) copy-start(bf16[1024,256]{1,0:T(8,128)(2,1)} %get-tuple-element.10.col_ref) | copy-start | bytes 1572868
  60.2 1.2 %copy-start.4 = (bf16[2048,256]{1,0:T(8,128)(2,1)S(1)}, bf16[2048,256]{1,0:T(8,128)(2,1)}, u32[]{:S(2)}) copy-start(bf16[2048,256]{1,0:T(8,128)(2,1)} %get-tuple-element.11.panel_ref) | copy-start | bytes 3145732
  61.4 0.8 %copy-start.5 = (f32[8,2048]{1,0:T(8,128)S(1)}, f32[8,2048]{1,0:T(8,128)}, u32[]{:S(2)}) copy-start(f32[8,2048]{1,0:T(8,128)} %get-tuple-element.12.norm_ref) | copy-start | bytes 196612
  62.2 7.8 %copy-start.1 = (bf16[1024,2048]{1,0:T(8,128)(2,1)S(1)}, bf16[1024,2048]{1,0:T(8,128)(2,1)}, u32[]{:S(2)}) copy-start(bf16[1024,2048]{1,0:T(8,128)(2,1)} %get-tuple-element.9.mine_hbm) | copy-start | bytes 12582916
  62.2 7.8 %copy-start.2 = (bf16[2048,256]{1,0:T(8,128)(2,1)S(1)}, bf16[2048,256]{1,0:T(8,128)(2,1)}, u32[]{:S(2)}) copy-start(bf16[2048,256]{1,0:T(8,128)(2,1)} %get-tuple-element.14.row_ref) | copy-start | bytes 3145732

commit v3 on v2

v3 whole, which is shorter than its diff:
```python
import functools
import math

import jax
import jax.numpy as jnp
from jax import lax
from jax.experimental import pallas as pl
from jax.experimental.pallas import tpu as pltpu
from jax.sharding import PartitionSpec as P

BF16, F32 = jnp.bfloat16, jnp.float32
MIB = 1 << 20
LANES = 128
WIDE = 256
PIECE = 1024


def nt_dot(left, right):
    return lax.dot_general(left, right, (((1,), (1,)), ((), ())), preferred_element_type=F32)


def split_squares(rows):
    wide = rows.astype(F32)
    square = wide * wide
    high = square.astype(BF16)
    return high, (square - high.astype(F32)).astype(BF16)


def row_norms(rows, scale):
    high, low = split_squares(rows)
    ones = jnp.ones((LANES, rows.shape[1]), BF16)
    return scale * (nt_dot(high, ones) + nt_dot(low, ones))


def lane_norms(rows, scale):
    high, low = split_squares(rows)
    ones = jnp.ones((8, rows.shape[1]), BF16)
    return scale * (nt_dot(ones, high) + nt_dot(ones, low))


def gauss(scale, inner, norms, other_norms):
    norms = jnp.concatenate([norms] * (inner.shape[1] // LANES), 1)
    return jnp.exp2(2.0 * scale * inner - norms - other_norms)


def start_load(teacher, inverse, inverse_out, pieces, sems, inverse_sems):
    copies = [
        pltpu.make_async_copy(teacher.at[pl.ds(i * PIECE, PIECE)], pieces.at[i], sems.at[i])
        for i in range(pieces.shape[0])
    ]
    inverse_copies = []
    for i in range(inverse.shape[0] // WIDE):
        at = (pl.ds(i * WIDE, WIDE), pl.ds(0, (i + 1) * WIDE))
        inverse_copies.append(pltpu.make_async_copy(inverse.at[at], inverse_out.at[at], inverse_sems.at[i]))
    for copy in copies + inverse_copies:
        copy.start()
    return copies, inverse_copies


def widen(copies, pieces, left, right):
    for i, copy in enumerate(copies):
        copy.wait()

        def step(part, carry):
            at = pl.ds(pl.multiple_of(part * WIDE, WIDE), WIDE)
            to = pl.ds(pl.multiple_of(i * PIECE + part * WIDE, WIDE), WIDE)
            left[to, :] = pieces[i, at, :LANES].astype(F32)
            right[to, :] = pieces[i, at, LANES:].astype(F32)
            return carry

        lax.fori_loop(0, PIECE // WIDE, step, 0)


def rows_kernel(scale, n_sets, teacher, inverse, panel_ids, row_ids, col_ids,
                half_out, panel_out, norm_out, col_out, inverse_ref,
                pieces, left, right, stage_left, stage_right, norms, cross, ids, sems, piece_sems, inverse_sems):
    row_at, col_at = lax.axis_index("row"), lax.axis_index("col")
    n_panel, n_rows, n_cols = n_sets
    copies = [
        pltpu.make_async_copy(panel_ids.at[pl.ds(0, n_panel), 1], ids.at[pl.ds(0, n_panel)], sems.at[0]),
        pltpu.make_async_copy(row_ids.at[:, row_at, 0], ids.at[pl.ds(n_panel, n_rows)], sems.at[1]),
        pltpu.make_async_copy(col_ids.at[:, col_at, 0], ids.at[pl.ds(n_panel + n_rows, n_cols)], sems.at[2]),
    ]
    for copy in copies:
        copy.start()
    piece_copies, inverse_copies = start_load(teacher, inverse, inverse_ref, pieces, piece_sems, inverse_sems)
    widen(piece_copies, pieces, left, right)
    for copy in copies:
        copy.wait()
    stretch = ids.shape[2]
    width = panel_out.shape[0]

    def gather(id_block, out, at, column, slot):
        for u in range(stretch):
            row = ids[id_block, 0, u]
            stage_left[slot, u : u + 1, :] = left[pl.ds(row, 1), :]
            stage_right[slot, u : u + 1, :] = right[pl.ds(row, 1), :]
        to = pl.ds(pl.multiple_of(at, stretch), stretch)
        out[to, column : column + LANES] = stage_left[slot].astype(BF16)
        out[to, column + LANES : column + 2 * LANES] = stage_right[slot].astype(BF16)

    def gather_pairs(id_pair, count, out, column):
        def one(i, carry):
            for b in range(2):
                gather(id_pair(i) + b, out, (2 * i + b) * stretch, column, b)
            return carry

        lax.fori_loop(0, count // 2, one, 0)

    gather_pairs(lambda i: n_panel + 4 * i + 2 * (col_at % 2), n_rows // 2, half_out, width)
    gather_pairs(lambda i: 2 * i, n_panel, panel_out, 0)
    gather_pairs(lambda i: n_panel + n_rows + 2 * i, n_cols, col_out, 0)
    norms[...] = row_norms(half_out[:, width:], scale)
    for at in range(0, width, WIDE):
        norm_out[:, at : at + WIDE] = lane_norms(panel_out[at : at + WIDE, :], scale)
    for copy in inverse_copies:
        copy.wait()
    cross_rows(scale, lambda: half_out[:, width:], norms, panel_out, norm_out, cross)
    for j in range(width // WIDE):
        factor_columns(j, inverse_ref, cross, half_out)


def cross_rows(scale, rows, norms, panel_ref, norm_ref, cross):
    for at in range(0, panel_ref.shape[0], WIDE):
        to = slice(at, at + WIDE)
        cross[:, to] = gauss(scale, nt_dot(rows(), panel_ref[to, :]), norms[...], norm_ref[:1, to]).astype(BF16)


def factor_columns(j, inverse_ref, cross, factor_ref):
    to, depth = slice(j * WIDE, (j + 1) * WIDE), (j + 1) * WIDE
    factor_ref[:, to] = nt_dot(cross[:, :depth], inverse_ref[to, :depth]).astype(BF16)


def column_kernel(scale, stretch, col_ref, panel_ref, norm_ref, inverse_ref, factor_out, own_out, norms, cross, sems):
    norms[...] = row_norms(col_ref[...], scale)
    cross_rows(scale, lambda: col_ref[...], norms, panel_ref, norm_ref, cross)
    own = pl.ds(pl.multiple_of(lax.axis_index("row") * stretch, stretch), stretch)
    n_steps = panel_ref.shape[0] // WIDE
    copies = []
    for j in range(n_steps):
        factor_columns(j, inverse_ref, cross, factor_out)
        to = pl.ds(j * WIDE, WIDE)
        copies.append(pltpu.make_async_copy(factor_out.at[own, to], own_out.at[:, to], sems.at[j]))
        copies[-1].start()
    for copy in copies:
        copy.wait()


def update_kernel(scale, n_row, n_col, stretch, mine, other, factor_ref, col_ref, out_hbm,
                  stage, norms, row_norm, out_sems):
    row_at, col_at = lax.axis_index("row"), lax.axis_index("col")
    parity = col_at % 2
    width = factor_ref.shape[1]
    tile = 2 * stretch
    n_cols = factor_ref.shape[0]
    for at in range(0, n_cols, WIDE):
        norms[:, at : at + WIDE] = lane_norms(col_ref[at : at + WIDE, :], scale)
    above = lax.broadcasted_iota(jnp.int32, (tile, LANES), 0)
    above = above // stretch * (n_row * stretch) + above % stretch - lax.broadcasted_iota(jnp.int32, (tile, LANES), 1)
    puts = []
    for step in range(mine.shape[0] // tile)[::-1]:
        here = slice(step * tile, (step + 1) * tile)
        blocks = min(n_row, ((4 * step + 3) * n_row + n_row - 1) // n_col + 1)
        blocks = -(-blocks * LANES // WIDE) * (WIDE // LANES)
        for half, other_half in ((mine, 0), (other, 1)):
            q = 4 * step + 2 * (parity if other_half == 0 else 1 - parity)
            first_row = (q * n_row + row_at) * stretch
            slot = len(puts)
            row_norm[...] = row_norms(half[here, width:], scale)
            for at in range(0, blocks * LANES, WIDE):
                to = slice(at, at + WIDE)
                update = nt_dot(half[here, :width], factor_ref[to, :])
                inner = nt_dot(half[here, width:], col_ref[to, :])
                result = gauss(scale, inner, row_norm[...], norms[:1, to]) - update
                for b in range(WIDE // LANES):
                    block = at // LANES + b
                    first_col = (block * n_col + col_at) * stretch
                    piece = result[:, b * LANES : (b + 1) * LANES]
                    piece = jnp.where(above >= first_col - first_row, piece, 0.0)
                    stage[slot, pl.ds(block, tile, stride=n_row), :] = piece
            for block in range(blocks, n_row):
                stage[slot, pl.ds(block, tile, stride=n_row), :] = jnp.zeros((tile, LANES), F32)
            to = pl.ds(pl.multiple_of(q * (stretch * n_row), stretch * n_row), tile * n_row)
            puts.append(pltpu.make_async_copy(stage.at[slot], out_hbm.at[to], out_sems.at[slot]))
            puts[-1].start()
    for put in puts:
        put.wait()


def shards(teacher, panel_ids, rest_ids, inverse):
    n_row, n_col = lax.axis_size("row"), lax.axis_size("col")
    stretch = rest_ids.shape[2]
    width = inverse.shape[0]
    emb = teacher.shape[1]
    n_rows, n_cols = n_col * stretch, n_row * stretch
    half = n_rows // 2
    scale = 2.0 / emb * math.log2(math.e)
    vmem = pl.BlockSpec(memory_space=pltpu.VMEM)
    hbm = pl.BlockSpec(memory_space=pl.ANY)
    near = functools.partial(pltpu.with_memory_space_constraint, memory_space=pltpu.VMEM)
    far = functools.partial(pltpu.with_memory_space_constraint, memory_space=pltpu.HBM)
    both = jnp.concatenate([rest_ids.reshape(1, 1, -1), panel_ids.reshape(1, 1, -1)], 0)
    both = jnp.broadcast_to(both[None], (n_row * n_col, *both.shape))
    both = lax.all_to_all(both, ("row", "col"), 0, 0, tiled=True)

    mine, panel_emb, panel_norms, col_emb, inverse_near = pl.pallas_call(
        functools.partial(rows_kernel, scale, (n_col, n_col, n_row)),
        out_shape=(
            pltpu.VMEM((half, width + emb), BF16),
            pltpu.VMEM((width, emb), BF16),
            pltpu.VMEM((8, width), F32),
            pltpu.VMEM((n_cols, emb), BF16),
            pltpu.VMEM((width, width), BF16),
        ),
        in_specs=[hbm] * 5,
        out_specs=[vmem] * 5,
        scratch_shapes=[
            pltpu.VMEM((teacher.shape[0] // PIECE, PIECE, emb), BF16),
            pltpu.VMEM((teacher.shape[0], LANES), F32),
            pltpu.VMEM((teacher.shape[0], LANES), F32),
            pltpu.VMEM((2, stretch, LANES), F32),
            pltpu.VMEM((2, stretch, LANES), F32),
            pltpu.VMEM((half, LANES), F32),
            pltpu.VMEM((half, width), BF16),
            pltpu.SMEM((2 * n_col + n_row, 1, stretch), jnp.int32),
            pltpu.SemaphoreType.DMA((3,)),
            pltpu.SemaphoreType.DMA((teacher.shape[0] // PIECE,)),
            pltpu.SemaphoreType.DMA((width // WIDE,)),
        ],
        compiler_params=pltpu.CompilerParams(vmem_limit_bytes=38 * MIB),
        name="rows",
    )(far(teacher), far(inverse), both, both.reshape(n_col, n_row, 2, 1, stretch),
      both.reshape(n_row, n_col, 2, 1, stretch))

    other = lax.ppermute(mine, "col", [(i, i ^ 1) for i in range(n_col)])

    factors, own = pl.pallas_call(
        functools.partial(column_kernel, scale, stretch),
        out_shape=(
            pltpu.VMEM((n_cols, width), BF16),
            jax.ShapeDtypeStruct((stretch, width), BF16),
        ),
        in_specs=[vmem] * 4,
        out_specs=[vmem, hbm],
        scratch_shapes=[
            pltpu.VMEM((n_cols, LANES), F32),
            pltpu.VMEM((n_cols, width), BF16),
            pltpu.SemaphoreType.DMA((width // WIDE,)),
        ],
        compiler_params=pltpu.CompilerParams(vmem_limit_bytes=14 * MIB),
        cost_estimate=pl.CostEstimate(
            flops=2 * n_cols * width * width, bytes_accessed=16 * MIB, transcendentals=n_cols * width),
        name="columns",
    )(near(col_emb), near(panel_emb), near(panel_norms), near(inverse_near))

    trailing = pl.pallas_call(
        functools.partial(update_kernel, scale, n_row, n_col, stretch),
        out_shape=jax.ShapeDtypeStruct((n_rows * n_row, stretch), F32),
        in_specs=[vmem] * 4,
        out_specs=hbm,
        scratch_shapes=[
            pltpu.VMEM((n_col // 2, 2 * stretch * n_row, stretch), F32),
            pltpu.VMEM((8, n_cols), F32),
            pltpu.VMEM((2 * stretch, LANES), F32),
            pltpu.SemaphoreType.DMA((n_col // 2,)),
        ],
        compiler_params=pltpu.CompilerParams(vmem_limit_bytes=20 * MIB),
        name="update",
    )(near(mine), near(other), near(factors), near(col_emb))
    return (
        trailing.reshape(n_col, 1, stretch, n_row, 1, stretch),
        own.reshape(1, 1, stretch, width),
    )


def solution(mesh):
    return jax.shard_map(
        shards,
        mesh=mesh,
        in_specs=(P(), P("col"), P("row", "col", None), P()),
        out_specs=(P(None, "row", None, None, "col", None), P("row", "col", None, None)),
        check_vma=False,
    )
```

time: 82.9 us -> 57.9 us (0.70)
  Pallas kernels: 52 us -> 33.9 us
  local copies, waits for them, and re-layouts: 6.56 us -> 0.07 us
    pallas_call x1, Pallas kernels: 31.8 us -> 16.9 us  [shards(): pl.pallas_call(functools.partial(rows_kernel, scale, (n_col, n_col, n_row...]
    unnamed x12 -> x0, local copies, waits for them, and re-layouts: 6.49 us -> none
    pallas_call x1, Pallas kernels: 12.4 us -> 9.39 us  [shards(): pl.pallas_call(functools.partial(update_kernel, scale, n_row, n_col, stre...]
  transfers between devices with their start and end apart: 1 -> 1, of which waited for: 0 -> 0; matrix products, arithmetic and copies ran while one was open for 0% -> 0% of each run, Pallas kernels for 9% -> 13%
where the time goes in v3:
time: 57.9 us; the launch traced here: 57.8 us
  Pallas kernels  33.9 us (59%)
  blocking collectives  21.7 us (37%)
  between operations  0.82 us (1%)
  other arithmetic  0.67 us (1%)
  starting transfers between devices  0.65 us (1%)
    all_to_all x1, blocking collectives, shards(): both = lax.all_to_all(both, ('row', 'col'), 0, 0, tiled=True)  21.7 us
    pallas_call x1, Pallas kernels, shards(): pl.pallas_call(functools.partial(rows_kernel, scale, (n_col, n_col, n_row...  16.9 us
    pallas_call x1, Pallas kernels, shards(): pl.pallas_call(functools.partial(update_kernel, scale, n_row, n_col, stre...  9.39 us
    pallas_call x1, Pallas kernels, shards(): pl.pallas_call(functools.partial(column_kernel, scale, stretch), out_shap...  7.62 us
  transfers between devices with their start and end apart: 1, of which 0 were waited for; matrix products, arithmetic and copies ran while one was open for 0% of the time, Pallas kernels for 13%

profile of v3, /device:TPU:1, one launch (start us, length us, event | category | flops | bytes accessed | tf_op | source)
XLA Modules:
  0.0 57.8 jit_solution(16641374892756526070)
XLA Ops:
  0.6 0.7 %pad_add_fusion = s32[2,1,128]{2,1,0:T(1,128)S(1)} fusion(s32[1,1,128]{2,1,0:T(1,128)} %bitcast.12, s32[1,1,128]{2,1,0:T(1,128)} %param.6), kind=kLoop, calls=%fused_computation | loop fusion | flops 256 | bytes 2048 | tf_op jit(solution)/shard_map/concatenate | solution.py:202
  1.3 0.1 broadcast_in_dim.9
  1.4 21.7 %all_to_all.5.panel_ids = s32[128,2,1,128]{3,2,1,0:T(1,128)S(1)} all-to-all(s32[128,2,1,128]{3,2,1,0:T(1,128)S(1)} %broadcast_in_dim.9), channel_id=1, replica_groups=mesh['row'=8,'col'=16] {'row','col'}, dimensions={0} | all-to-all | bytes 262144 | tf_op jit(solution)/shard_map/all_to_all | solution.py:204
  23.0 16.9 %rows.1 = (bf16[1024,2304]{1,0:T(8,128)(2,1)S(1)}, bf16[2048,256]{1,0:T(8,128)(2,1)S(1)}, f32[8,2048]{1,0:T(8,128)S(1)}, bf16[1024,256]{1,0:T(8,128)(2,1)S(1)}, bf16[2048,2048]{1,0:T(8,128)(2,1)S(1)}) custom-call(bf16[16384,256]{1,0:T(8,128)(2,1)} %teacher.1, bf16[2048,2048]{1,0:T(8,128)(2,1)} %inverse.1, s32[128,2,1,128]{3,2,1,0:T(1,128)S(1)} %all_to_all.5.panel_ids, ...), custom_call_target="tpu_custom_call" | custom-call | tf_op jit(solution)/shard_map/rows/pallas_call | solution.py:206
  40.0 0.7 %collective-permute-start = (bf16[1024,2304]{1,0:T(8,128)(2,1)S(1)}, bf16[1024,2304]{1,0:T(8,128)(2,1)S(1)}, u32[]{:S(2)}, u32[]{:S(2)}) collective-permute-start(bf16[1024,2304]{1,0:T(8,128)(2,1)S(1)} %get-tuple-element.9.mine), channel_id=1, source_target_pairs={{0,1},{1,0},{2,3},{3,2},{4,5},{5,4},{6,7},{7,6},{8,9},{9,8},{10,11... | collective-permute-start | bytes 14155784 | tf_op jit(solution)/shard_map/ppermute | solution.py:235
  40.6 7.6 %columns.1 = (bf16[1024,2048]{1,0:T(8,128)(2,1)S(1)}, bf16[128,2048]{1,0:T(8,128)(2,1)}) custom-call(bf16[1024,256]{1,0:T(8,128)(2,1)S(1)} %get-tuple-element.10.col_ref, bf16[2048,256]{1,0:T(8,128)(2,1)S(1)} %get-tuple-element.11.panel_ref, f32[8,2048]{1,0:T(8,128)S(1)} %get-tuple-element.12.norm_ref, bf16[2048,2048]{1,0:T(8,128)(2,1)S(1)} %get-tuple-element.13.inverse_ref), custom_call_target="tpu_custom_call" | custom-call | flops 8589934592 | bytes 16777216 | tf_op jit(solution)/shard_map/columns/pallas_call | solution.py:237
  48.2 0.0 collective-permute-done.other
  48.3 9.4 %update.1 = f32[16384,128]{1,0:T(8,128)} custom-call(bf16[1024,2304]{1,0:T(8,128)(2,1)S(1)} %get-tuple-element.9.mine, bf16[1024,2304]{1,0:T(8,128)(2,1)S(1)} %collective-permute-done.other, bf16[1024,2048]{1,0:T(8,128)(2,1)S(1)} %get-tuple-element.14.factor_ref, bf16[1024,256]{1,0:T(8,128)(2,1)S(1)} %get-tuple-element.10.col_ref), custom_call_target="tpu_custom_call" | custom-call | tf_op jit(solution)/shard_map/update/pallas_call | solution.py:256
Async XLA Ops:
  40.0 8.3 %collective-permute-start = (bf16[1024,2304]{1,0:T(8,128)(2,1)S(1)}, bf16[1024,2304]{1,0:T(8,128)(2,1)S(1)}, u32[]{:S(2)}, u32[]{:S(2)}) collective-permute-start(bf16[1024,2304]{1,0:T(8,128)(2,1)S(1)} %get-tuple-element.9.mine), channel_id=1, source_target_pairs={{0,1},{1,0},{2,3},{3,2},{4,5},{5,4},{6,7},{7,6},{8,9},{9,8},{10,11... | collective-permute-start | bytes 14155784 | tf_op jit(solution)/shard_map/ppermute | solution.py:235

commit v4 on v3

v4 whole, which is shorter than its diff:
```python
import functools
import math

import jax
import jax.numpy as jnp
from jax import lax
from jax.experimental import pallas as pl
from jax.experimental.pallas import tpu as pltpu
from jax.sharding import PartitionSpec as P

BF16, F32 = jnp.bfloat16, jnp.float32
MIB = 1 << 20
LANES = 128
WIDE = 256
PIECE = 1024


def nt_dot(left, right):
    return lax.dot_general(left, right, (((1,), (1,)), ((), ())), preferred_element_type=F32)


def split_squares(rows):
    wide = rows.astype(F32)
    square = wide * wide
    high = square.astype(BF16)
    return high, (square - high.astype(F32)).astype(BF16)


def row_norms(rows, scale):
    high, low = split_squares(rows)
    ones = jnp.ones((LANES, rows.shape[1]), BF16)
    return scale * (nt_dot(high, ones) + nt_dot(low, ones))


def lane_norms(rows, scale):
    high, low = split_squares(rows)
    ones = jnp.ones((8, rows.shape[1]), BF16)
    return scale * (nt_dot(ones, high) + nt_dot(ones, low))


def gauss(scale, inner, norms, other_norms):
    norms = jnp.concatenate([norms] * (inner.shape[1] // LANES), 1)
    return jnp.exp2(2.0 * scale * inner - norms - other_norms)


def start_load(teacher, inverse, inverse_out, pieces, sems, inverse_sems):
    copies = [
        pltpu.make_async_copy(teacher.at[pl.ds(i * PIECE, PIECE)], pieces.at[i], sems.at[i])
        for i in range(pieces.shape[0])
    ]
    inverse_copies = []
    for i in range(inverse.shape[0] // WIDE):
        at = (pl.ds(i * WIDE, WIDE), pl.ds(0, (i + 1) * WIDE))
        inverse_copies.append(pltpu.make_async_copy(inverse.at[at], inverse_out.at[at], inverse_sems.at[i]))
    for copy in copies:
        copy.start()
    return copies, inverse_copies


def widen(copies, pieces, left, right):
    for i, copy in enumerate(copies):
        copy.wait()

        def step(part, carry):
            at = pl.ds(pl.multiple_of(part * WIDE, WIDE), WIDE)
            to = pl.ds(pl.multiple_of(i * PIECE + part * WIDE, WIDE), WIDE)
            left[to, :] = pieces[i, at, :LANES].astype(F32)
            right[to, :] = pieces[i, at, LANES:].astype(F32)
            return carry

        lax.fori_loop(0, PIECE // WIDE, step, 0)


def gather_blocks(ids, tables, stages, id_block, count, out, column):
    stretch, slots = ids.shape[2], stages[0].shape[0]

    def one(i, carry):
        for b in range(slots):
            block = id_block(i, b)
            for u in range(stretch):
                row = ids[block, 0, u]
                for table, stage in zip(tables, stages):
                    stage[b, u : u + 1, :] = table[pl.ds(row, 1), :]
            to = pl.ds(pl.multiple_of((slots * i + b) * stretch, stretch), stretch)
            for k, stage in enumerate(stages):
                out[to, column + k * LANES : column + (k + 1) * LANES] = stage[b].astype(BF16)
        return carry

    lax.fori_loop(0, count // slots, one, 0)


def rows_kernel(scale, n_sets, teacher, inverse, panel_ids, row_ids, col_ids,
                half_out, panel_out, norm_out, col_out, inverse_ref, norms,
                pieces, left, right, stage_left, stage_right, cross, ids, sems, piece_sems, inverse_sems):
    row_at, col_at = lax.axis_index("row"), lax.axis_index("col")
    n_panel, n_rows, n_cols = n_sets
    copies = [
        pltpu.make_async_copy(panel_ids.at[pl.ds(0, n_panel), 1], ids.at[pl.ds(0, n_panel)], sems.at[0]),
        pltpu.make_async_copy(row_ids.at[:, row_at, 0], ids.at[pl.ds(n_panel, n_rows)], sems.at[1]),
        pltpu.make_async_copy(col_ids.at[:, col_at, 0], ids.at[pl.ds(n_panel + n_rows, n_cols)], sems.at[2]),
    ]
    for copy in copies:
        copy.start()
    piece_copies, inverse_copies = start_load(teacher, inverse, inverse_ref, pieces, piece_sems, inverse_sems)
    widen(piece_copies, pieces, left, right)
    for copy in inverse_copies:
        copy.start()
    for copy in copies:
        copy.wait()
    width = panel_out.shape[0]

    take = functools.partial(gather_blocks, ids, (left, right), (stage_left, stage_right))
    slots = stage_left.shape[0]
    take(lambda i, b: n_panel + 2 * slots * i + 4 * (b // 2) + b % 2 + 2 * (col_at % 2), n_rows // 2, half_out, width)
    take(lambda i, b: slots * i + b, n_panel, panel_out, 0)
    take(lambda i, b: n_panel + n_rows + slots * i + b, n_cols, col_out, 0)
    norms[...] = row_norms(half_out[:, width:], scale)
    for at in range(0, width, WIDE):
        norm_out[:, at : at + WIDE] = lane_norms(panel_out[at : at + WIDE, :], scale)
    for copy in inverse_copies:
        copy.wait()
    cross_rows(scale, lambda: half_out[:, width:], norms, panel_out, norm_out, cross)
    for j in range(width // WIDE):
        factor_columns(j, inverse_ref, cross, half_out)


def cross_rows(scale, rows, norms, panel_ref, norm_ref, cross):
    for at in range(0, panel_ref.shape[0], WIDE):
        to = slice(at, at + WIDE)
        cross[:, to] = gauss(scale, nt_dot(rows(), panel_ref[to, :]), norms[...], norm_ref[:1, to]).astype(BF16)


def factor_columns(j, inverse_ref, cross, factor_ref):
    to, depth = slice(j * WIDE, (j + 1) * WIDE), (j + 1) * WIDE
    factor_ref[:, to] = nt_dot(cross[:, :depth], inverse_ref[to, :depth]).astype(BF16)


def column_kernel(scale, n_row, n_col, stretch, col_ref, panel_ref, norm_ref, inverse_ref, mine, mine_norms,
                  factor_out, col_norms, first_out, norms, cross):
    norms[...] = row_norms(col_ref[...], scale)
    for at in range(0, col_ref.shape[0], WIDE):
        col_norms[:, at : at + WIDE] = lane_norms(col_ref[at : at + WIDE, :], scale)
    cross_rows(scale, lambda: col_ref[...], norms, panel_ref, norm_ref, cross)
    for j in range(panel_ref.shape[0] // WIDE):
        factor_columns(j, inverse_ref, cross, factor_out)
    step = mine.shape[0] // (2 * stretch) - 1
    update_tile(scale, n_row, n_col, stretch, step, lax.axis_index("col") % 2, mine, mine_norms,
                factor_out, col_ref, col_norms, first_out)


def update_tile(scale, n_row, n_col, stretch, step, pair, half, row_norm, factor_ref, col_ref, norms, stage):
    row_at, col_at = lax.axis_index("row"), lax.axis_index("col")
    width, tile = factor_ref.shape[1], 2 * stretch
    here = slice(step * tile, (step + 1) * tile)
    first_row = ((4 * step + 2 * pair) * n_row + row_at) * stretch
    above = lax.broadcasted_iota(jnp.int32, (tile, LANES), 0)
    above = above // stretch * (n_row * stretch) + above % stretch - lax.broadcasted_iota(jnp.int32, (tile, LANES), 1)
    blocks = min(n_row, ((4 * step + 3) * n_row + n_row - 1) // n_col + 1)
    blocks = -(-blocks * LANES // WIDE) * (WIDE // LANES)
    for at in range(0, blocks * LANES, WIDE):
        to = slice(at, at + WIDE)
        update = nt_dot(half[here, :width], factor_ref[to, :])
        inner = nt_dot(half[here, width:], col_ref[to, :])
        result = gauss(scale, inner, row_norm[here, :], norms[:1, to]) - update
        for b in range(WIDE // LANES):
            block = at // LANES + b
            first_col = (block * n_col + col_at) * stretch
            piece = result[:, b * LANES : (b + 1) * LANES]
            piece = jnp.where(above >= first_col - first_row, piece, 0.0)
            stage[pl.ds(block, tile, stride=n_row), :] = piece
    for block in range(blocks, n_row):
        stage[pl.ds(block, tile, stride=n_row), :] = jnp.zeros((tile, LANES), F32)


def update_kernel(scale, n_row, n_col, stretch, mine, other, factor_ref, col_ref, mine_norms, norms, first,
                  out_hbm, own_out, stage, other_norms, out_sems, own_sem):
    parity = lax.axis_index("col") % 2
    width = factor_ref.shape[1]
    size = first.shape[0]
    own = pl.ds(pl.multiple_of(lax.axis_index("row") * stretch, stretch), stretch)
    puts = []

    def put(step, pair, ref):
        at = (4 * step + 2 * pair) * (stretch * n_row)
        to = pl.ds(pl.multiple_of(at, stretch * n_row), size)
        puts.append(pltpu.make_async_copy(ref, out_hbm.at[to], out_sems.at[len(puts)]))
        puts[-1].start()

    steps = mine.shape[0] // (2 * stretch)
    put(steps - 1, parity, first)
    own_copy = pltpu.make_async_copy(factor_ref.at[own], own_out, own_sem)
    own_copy.start()
    other_norms[...] = row_norms(other[:, width:], scale)
    for step in range(steps)[::-1]:
        for pair, half, row_norm in ((parity, mine, mine_norms), (1 - parity, other, other_norms)):
            if step == steps - 1 and half is mine:
                continue
            slot = stage.at[len(puts) - 1]
            update_tile(scale, n_row, n_col, stretch, step, pair, half, row_norm, factor_ref, col_ref, norms, slot)
            put(step, pair, slot)
    own_copy.wait()
    for copy in puts:
        copy.wait()


def shards(teacher, panel_ids, rest_ids, inverse):
    n_row, n_col = lax.axis_size("row"), lax.axis_size("col")
    stretch = rest_ids.shape[2]
    width = inverse.shape[0]
    emb = teacher.shape[1]
    n_rows, n_cols = n_col * stretch, n_row * stretch
    half = n_rows // 2
    scale = 2.0 / emb * math.log2(math.e)
    vmem = pl.BlockSpec(memory_space=pltpu.VMEM)
    hbm = pl.BlockSpec(memory_space=pl.ANY)
    near = functools.partial(pltpu.with_memory_space_constraint, memory_space=pltpu.VMEM)
    far = functools.partial(pltpu.with_memory_space_constraint, memory_space=pltpu.HBM)
    wide = (n_row * n_col, 2, 1, stretch)
    which = lax.broadcasted_iota(jnp.int32, wide, 1)
    both = jnp.where(which == 0, rest_ids.reshape(1, 1, 1, -1), panel_ids.reshape(1, 1, 1, -1))
    both = lax.all_to_all(both, ("row", "col"), 0, 0, tiled=True)

    n_table = teacher.shape[0]
    mine, panel_emb, panel_norms, col_emb, inverse_near, mine_norms = pl.pallas_call(
        functools.partial(rows_kernel, scale, (n_col, n_col, n_row)),
        out_shape=(
            pltpu.VMEM((half, width + emb), BF16),
            pltpu.VMEM((width, emb), BF16),
            pltpu.VMEM((8, width), F32),
            pltpu.VMEM((n_cols, emb), BF16),
            pltpu.VMEM((width, width), BF16),
            pltpu.VMEM((half, LANES), F32),
        ),
        in_specs=[hbm] * 5,
        out_specs=[vmem] * 6,
        scratch_shapes=[
            pltpu.VMEM((n_table // PIECE, PIECE, emb), BF16),
            pltpu.VMEM((n_table, LANES), F32),
            pltpu.VMEM((n_table, LANES), F32),
            pltpu.VMEM((4, stretch, LANES), F32),
            pltpu.VMEM((4, stretch, LANES), F32),
            pltpu.VMEM((half, width), BF16),
            pltpu.SMEM((2 * n_col + n_row, 1, stretch), jnp.int32),
            pltpu.SemaphoreType.DMA((3,)),
            pltpu.SemaphoreType.DMA((n_table // PIECE,)),
            pltpu.SemaphoreType.DMA((width // WIDE,)),
        ],
        compiler_params=pltpu.CompilerParams(vmem_limit_bytes=36 * MIB),
        name="rows",
    )(far(teacher), far(inverse), both, both.reshape(n_col, n_row, 2, 1, stretch),
      both.reshape(n_row, n_col, 2, 1, stretch))

    other = lax.ppermute(mine, "col", [(i, i ^ 1) for i in range(n_col)])

    size = 2 * stretch * n_row
    factors, col_norms, first = pl.pallas_call(
        functools.partial(column_kernel, scale, n_row, n_col, stretch),
        out_shape=(
            pltpu.VMEM((n_cols, width), BF16),
            pltpu.VMEM((8, n_cols), F32),
            pltpu.VMEM((size, stretch), F32),
        ),
        in_specs=[vmem] * 6,
        out_specs=[vmem] * 3,
        scratch_shapes=[
            pltpu.VMEM((n_cols, LANES), F32),
            pltpu.VMEM((n_cols, width), BF16),
        ],
        compiler_params=pltpu.CompilerParams(vmem_limit_bytes=14 * MIB),
        cost_estimate=pl.CostEstimate(
            flops=2 * n_cols * width * width, bytes_accessed=16 * MIB, transcendentals=n_cols * width),
        name="columns",
    )(near(col_emb), near(panel_emb), near(panel_norms), near(inverse_near), near(mine), near(mine_norms))

    trailing, own = pl.pallas_call(
        functools.partial(update_kernel, scale, n_row, n_col, stretch),
        out_shape=(
            jax.ShapeDtypeStruct((n_rows * n_row, stretch), F32),
            jax.ShapeDtypeStruct((stretch, width), BF16),
        ),
        in_specs=[vmem] * 7,
        out_specs=[hbm] * 2,
        scratch_shapes=[
            pltpu.VMEM((n_col // 2 - 1, size, stretch), F32),
            pltpu.VMEM((half, LANES), F32),
            pltpu.SemaphoreType.DMA((n_col // 2,)),
            pltpu.SemaphoreType.DMA,
        ],
        compiler_params=pltpu.CompilerParams(vmem_limit_bytes=20 * MIB),
        name="update",
    )(near(mine), near(other), near(factors), near(col_emb), near(mine_norms), near(col_norms), near(first))
    return (
        trailing.reshape(n_col, 1, stretch, n_row, 1, stretch),
        own.reshape(1, 1, stretch, width),
    )


def solution(mesh):
    return jax.shard_map(
        shards,
        mesh=mesh,
        in_specs=(P(), P("col"), P("row", "col", None), P()),
        out_specs=(P(None, "row", None, None, "col", None), P("row", "col", None, None)),
        check_vma=False,
    )
```

time: 57.9 us -> 56.1 us (0.969)
  Pallas kernels: 33.9 us -> 32 us
    pallas_call x1, Pallas kernels: 9.39 us -> 7.63 us  [shards(): pl.pallas_call(functools.partial(update_kernel, scale, n_row, n_col, stre...]
    pallas_call x1, Pallas kernels: 16.9 us -> 15.7 us  [shards(): pl.pallas_call(functools.partial(rows_kernel, scale, (n_col, n_col, n_row...]
    pallas_call x1, Pallas kernels: 7.62 us -> 8.67 us  [shards(): pl.pallas_call(functools.partial(column_kernel, scale, n_row, n_col, stre...]
    select_n x0 -> x1, other arithmetic: none -> 0.81 us  [shards(): jnp.where(which == 0, rest_ids.reshape(1, 1, 1, -1), panel_ids.reshape(1,...]
    concatenate x1 -> x0, other arithmetic: 0.67 us -> none  [shards(): jnp.concatenate([rest_ids.reshape(1, 1, -1), panel_ids.reshape(1, 1, -1)]...]
  transfers between devices with their start and end apart: 1 -> 1, of which waited for: 0 -> 0; matrix products, arithmetic and copies ran while one was open for 0% -> 0% of each run, Pallas kernels for 13% -> 16%
where the time goes in v4:
time: 56.1 us; the launch traced here: 55.9 us
  Pallas kernels  32 us (57%)
  blocking collectives  21.7 us (39%)
  between operations  0.83 us (1%)
  other arithmetic  0.82 us (1%)
  starting transfers between devices  0.66 us (1%)
    all_to_all x1, blocking collectives, shards(): both = lax.all_to_all(both, ('row', 'col'), 0, 0, tiled=True)  21.7 us
    pallas_call x1, Pallas kernels, shards(): pl.pallas_call(functools.partial(rows_kernel, scale, (n_col, n_col, n_row...  15.7 us
    pallas_call x1, Pallas kernels, shards(): pl.pallas_call(functools.partial(column_kernel, scale, n_row, n_col, stre...  8.67 us
    pallas_call x1, Pallas kernels, shards(): pl.pallas_call(functools.partial(update_kernel, scale, n_row, n_col, stre...  7.63 us
  transfers between devices with their start and end apart: 1, of which 0 were waited for; matrix products, arithmetic and copies ran while one was open for 0% of the time, Pallas kernels for 16%

profile of v4, /device:TPU:1, one launch (start us, length us, event | category | flops | bytes accessed | tf_op | source)
XLA Modules:
  0.0 55.9 jit_solution(2671862201190669023)
XLA Ops:
  0.6 0.8 %broadcast_select_fusion = s32[128,2,1,128]{3,2,1,0:T(1,128)S(1)} fusion(pred[2]{0:T(512)(128)(4,1)S(1)} %iota_compare_fusion, s32[128]{0:T(128)} %param.5, s32[128]{0:T(128)} %bitcast.9), kind=kLoop, calls=%fused_computation | loop fusion | flops 32768 | bytes 132098 | tf_op jit(solution)/shard_map/jit(_where)/select_n | solution.py:220
  1.5 21.7 %all_to_all.5.panel_ids = s32[128,2,1,128]{3,2,1,0:T(1,128)S(1)} all-to-all(s32[128,2,1,128]{3,2,1,0:T(1,128)S(1)} %broadcast_select_fusion), channel_id=1, replica_groups=mesh['row'=8,'col'=16] {'row','col'}, dimensions={0} | all-to-all | bytes 262144 | tf_op jit(solution)/shard_map/all_to_all | solution.py:221
  23.1 15.7 %rows.1 = (bf16[1024,2304]{1,0:T(8,128)(2,1)S(1)}, bf16[2048,256]{1,0:T(8,128)(2,1)S(1)}, f32[8,2048]{1,0:T(8,128)S(1)}, bf16[1024,256]{1,0:T(8,128)(2,1)S(1)}, ...) custom-call(bf16[16384,256]{1,0:T(8,128)(2,1)} %teacher.1, bf16[2048,2048]{1,0:T(8,128)(2,1)} %inverse.1, ...), custom_call_target="tpu_custom_call" | custom-call | tf_op jit(solution)/shard_map/rows/pallas_call | solution.py:224
  38.8 0.7 %collective-permute-start = (bf16[1024,2304]{1,0:T(8,128)(2,1)S(1)}, bf16[1024,2304]{1,0:T(8,128)(2,1)S(1)}, u32[]{:S(2)}, u32[]{:S(2)}) collective-permute-start(bf16[1024,2304]{1,0:T(8,128)(2,1)S(1)} %get-tuple-element.13.mine), channel_id=1, source_target_pairs={{0,1},{1,0},{2,3},{3,2},{4,5},{5,4},{6,7},{7,6},{8,9},{9,8},{10,11... | collective-permute-start | bytes 14155784 | tf_op jit(solution)/shard_map/ppermute | solution.py:253
  39.5 8.7 %columns.1 = (bf16[1024,2048]{1,0:T(8,128)(2,1)S(1)}, f32[8,1024]{1,0:T(8,128)S(1)}, f32[2048,128]{1,0:T(8,128)S(1)}) custom-call(bf16[1024,256]{1,0:T(8,128)(2,1)S(1)} %get-tuple-element.14.col_ref, bf16[2048,256]{1,0:T(8,128)(2,1)S(1)} %get-tuple-element.15.panel_ref, f32[8,2048]{1,0:T(8,128)S(1)} %get-tuple-element.16.norm_ref, ...), custom_call_target="tpu_custom_call" | custom-call | flops 8589934592 | bytes 16777216 | tf_op jit(solution)/shard_map/columns/pallas_call | solution.py:256
  48.1 0.0 collective-permute-done.other
  48.1 7.6 %update.1 = (f32[16384,128]{1,0:T(8,128)}, bf16[128,2048]{1,0:T(8,128)(2,1)}) custom-call(bf16[1024,2304]{1,0:T(8,128)(2,1)S(1)} %get-tuple-element.13.mine, bf16[1024,2304]{1,0:T(8,128)(2,1)S(1)} %collective-permute-done.other, bf16[1024,2048]{1,0:T(8,128)(2,1)S(1)} %get-tuple-element.19.factor_ref, bf16[1024,256]{1,0:T(8,128)(2,1)S(1)} %get-tuple-element.14.col_ref, ...), custom_call_target="tpu_custom_call" | custom-call | tf_op jit(solution)/shard_map/update/pallas_call | solution.py:275
  (1 shorter events, 0.0 us)
Async XLA Ops:
  38.8 9.3 %collective-permute-start = (bf16[1024,2304]{1,0:T(8,128)(2,1)S(1)}, bf16[1024,2304]{1,0:T(8,128)(2,1)S(1)}, u32[]{:S(2)}, u32[]{:S(2)}) collective-permute-start(bf16[1024,2304]{1,0:T(8,128)(2,1)S(1)} %get-tuple-element.13.mine), channel_id=1, source_target_pairs={{0,1},{1,0},{2,3},{3,2},{4,5},{5,4},{6,7},{7,6},{8,9},{9,8},{10,11... | collective-permute-start | bytes 14155784 | tf_op jit(solution)/shard_map/ppermute | solution.py:253

commit v5 on v4

--- a/solution.py
+++ b/solution.py
@@ -216,7 +216,7 @@
     near = functools.partial(pltpu.with_memory_space_constraint, memory_space=pltpu.VMEM)
     far = functools.partial(pltpu.with_memory_space_constraint, memory_space=pltpu.HBM)
     wide = (n_row * n_col, 2, 1, stretch)
-    which = lax.broadcasted_iota(jnp.int32, wide, 1)
+    which = lax.iota(jnp.int32, math.prod(wide)).reshape(wide) // stretch % 2
     both = jnp.where(which == 0, rest_ids.reshape(1, 1, 1, -1), panel_ids.reshape(1, 1, 1, -1))
     both = lax.all_to_all(both, ("row", "col"), 0, 0, tiled=True)
 
@@ -237,8 +237,8 @@
             pltpu.VMEM((n_table // PIECE, PIECE, emb), BF16),
             pltpu.VMEM((n_table, LANES), F32),
             pltpu.VMEM((n_table, LANES), F32),
-            pltpu.VMEM((4, stretch, LANES), F32),
-            pltpu.VMEM((4, stretch, LANES), F32),
+            pltpu.VMEM((8, stretch, LANES), F32),
+            pltpu.VMEM((8, stretch, LANES), F32),
             pltpu.VMEM((half, width), BF16),
             pltpu.SMEM((2 * n_col + n_row, 1, stretch), jnp.int32),
             pltpu.SemaphoreType.DMA((3,)),

time: 56.1 us -> 55.6 us (level)
  no operation moved by 1% of the time
where the time goes in v5:
time: 55.6 us; the launch traced here: 55.5 us
  Pallas kernels  31.5 us (57%)
  blocking collectives  21.7 us (39%)
  other arithmetic  0.86 us (2%)
  between operations  0.82 us (1%)
  starting transfers between devices  0.66 us (1%)
    all_to_all x1, blocking collectives, shards(): both = lax.all_to_all(both, ('row', 'col'), 0, 0, tiled=True)  21.7 us
    pallas_call x1, Pallas kernels, shards(): pl.pallas_call(functools.partial(rows_kernel, scale, (n_col, n_col, n_row...  15.2 us
    pallas_call x1, Pallas kernels, shards(): pl.pallas_call(functools.partial(column_kernel, scale, n_row, n_col, stre...  8.67 us
    pallas_call x1, Pallas kernels, shards(): pl.pallas_call(functools.partial(update_kernel, scale, n_row, n_col, stre...  7.63 us
  transfers between devices with their start and end apart: 1, of which 0 were waited for; matrix products, arithmetic and copies ran while one was open for 0% of the time, Pallas kernels for 16%

profile of v5, /device:TPU:1, one launch (start us, length us, event | category | flops | bytes accessed | tf_op | source)
XLA Modules:
  0.0 55.5 jit_solution(13048799441232372150)
XLA Ops:
  0.6 0.9 %compare_select_fusion.2 = s32[128,2,1,128]{3,2,1,0:T(1,128)S(1)} fusion(s32[128]{0:T(128)} %param.5, s32[128]{0:T(128)} %bitcast.9), kind=kLoop, calls=%fused_computation.2 | loop fusion | flops 1048576 | bytes 132096 | tf_op jit(solution)/shard_map/jit(_where)/select_n | solution.py:220
  1.5 21.7 %all_to_all.5.panel_ids = s32[128,2,1,128]{3,2,1,0:T(1,128)S(1)} all-to-all(s32[128,2,1,128]{3,2,1,0:T(1,128)S(1)} %compare_select_fusion.2), channel_id=1, replica_groups=mesh['row'=8,'col'=16] {'row','col'}, dimensions={0} | all-to-all | bytes 262144 | tf_op jit(solution)/shard_map/all_to_all | solution.py:221
  23.2 15.2 %rows.1 = (bf16[1024,2304]{1,0:T(8,128)(2,1)S(1)}, bf16[2048,256]{1,0:T(8,128)(2,1)S(1)}, f32[8,2048]{1,0:T(8,128)S(1)}, bf16[1024,256]{1,0:T(8,128)(2,1)S(1)}, ...) custom-call(bf16[16384,256]{1,0:T(8,128)(2,1)} %teacher.1, bf16[2048,2048]{1,0:T(8,128)(2,1)} %inverse.1, ...), custom_call_target="tpu_custom_call" | custom-call | tf_op jit(solution)/shard_map/rows/pallas_call | solution.py:224
  38.4 0.7 %collective-permute-start = (bf16[1024,2304]{1,0:T(8,128)(2,1)S(1)}, bf16[1024,2304]{1,0:T(8,128)(2,1)S(1)}, u32[]{:S(2)}, u32[]{:S(2)}) collective-permute-start(bf16[1024,2304]{1,0:T(8,128)(2,1)S(1)} %get-tuple-element.13.mine), channel_id=1, source_target_pairs={{0,1},{1,0},{2,3},{3,2},{4,5},{5,4},{6,7},{7,6},{8,9},{9,8},{10,11... | collective-permute-start | bytes 14155784 | tf_op jit(solution)/shard_map/ppermute | solution.py:253
  39.0 8.7 %columns.1 = (bf16[1024,2048]{1,0:T(8,128)(2,1)S(1)}, f32[8,1024]{1,0:T(8,128)S(1)}, f32[2048,128]{1,0:T(8,128)S(1)}) custom-call(bf16[1024,256]{1,0:T(8,128)(2,1)S(1)} %get-tuple-element.14.col_ref, bf16[2048,256]{1,0:T(8,128)(2,1)S(1)} %get-tuple-element.15.panel_ref, f32[8,2048]{1,0:T(8,128)S(1)} %get-tuple-element.16.norm_ref, ...), custom_call_target="tpu_custom_call" | custom-call | flops 8589934592 | bytes 16777216 | tf_op jit(solution)/shard_map/columns/pallas_call | solution.py:256
  47.7 0.0 collective-permute-done.other
  47.7 7.6 %update.1 = (f32[16384,128]{1,0:T(8,128)}, bf16[128,2048]{1,0:T(8,128)(2,1)}) custom-call(bf16[1024,2304]{1,0:T(8,128)(2,1)S(1)} %get-tuple-element.13.mine, bf16[1024,2304]{1,0:T(8,128)(2,1)S(1)} %collective-permute-done.other, bf16[1024,2048]{1,0:T(8,128)(2,1)S(1)} %get-tuple-element.19.factor_ref, bf16[1024,256]{1,0:T(8,128)(2,1)S(1)} %get-tuple-element.14.col_ref, ...), custom_call_target="tpu_custom_call" | custom-call | tf_op jit(solution)/shard_map/update/pallas_call | solution.py:275
Async XLA Ops:
  38.4 9.3 %collective-permute-start = (bf16[1024,2304]{1,0:T(8,128)(2,1)S(1)}, bf16[1024,2304]{1,0:T(8,128)(2,1)S(1)}, u32[]{:S(2)}, u32[]{:S(2)}) collective-permute-start(bf16[1024,2304]{1,0:T(8,128)(2,1)S(1)} %get-tuple-element.13.mine), channel_id=1, source_target_pairs={{0,1},{1,0},{2,3},{3,2},{4,5},{5,4},{6,7},{7,6},{8,9},{9,8},{10,11... | collective-permute-start | bytes 14155784 | tf_op jit(solution)/shard_map/ppermute | solution.py:253

commit v6 on v5

--- a/solution.py
+++ b/solution.py
@@ -144,8 +144,14 @@
     for j in range(panel_ref.shape[0] // WIDE):
         factor_columns(j, inverse_ref, cross, factor_out)
     step = mine.shape[0] // (2 * stretch) - 1
+    assert blocks_reached(step, n_row, n_col) == n_row
     update_tile(scale, n_row, n_col, stretch, step, lax.axis_index("col") % 2, mine, mine_norms,
                 factor_out, col_ref, col_norms, first_out)
+
+
+def blocks_reached(step, n_row, n_col):
+    blocks = min(n_row, ((4 * step + 3) * n_row + n_row - 1) // n_col + 1)
+    return -(-blocks * LANES // WIDE) * (WIDE // LANES)
 
 
 def update_tile(scale, n_row, n_col, stretch, step, pair, half, row_norm, factor_ref, col_ref, norms, stage):
@@ -155,8 +161,7 @@
     first_row = ((4 * step + 2 * pair) * n_row + row_at) * stretch
     above = lax.broadcasted_iota(jnp.int32, (tile, LANES), 0)
     above = above // stretch * (n_row * stretch) + above % stretch - lax.broadcasted_iota(jnp.int32, (tile, LANES), 1)
-    blocks = min(n_row, ((4 * step + 3) * n_row + n_row - 1) // n_col + 1)
-    blocks = -(-blocks * LANES // WIDE) * (WIDE // LANES)
+    blocks = blocks_reached(step, n_row, n_col)
     for at in range(0, blocks * LANES, WIDE):
         to = slice(at, at + WIDE)
         update = nt_dot(half[here, :width], factor_ref[to, :])
@@ -168,8 +173,6 @@
             piece = result[:, b * LANES : (b + 1) * LANES]
             piece = jnp.where(above >= first_col - first_row, piece, 0.0)
             stage[pl.ds(block, tile, stride=n_row), :] = piece
-    for block in range(blocks, n_row):
-        stage[pl.ds(block, tile, stride=n_row), :] = jnp.zeros((tile, LANES), F32)
 
 
 def update_kernel(scale, n_row, n_col, stretch, mine, other, factor_ref, col_ref, mine_norms, norms, first,
@@ -190,6 +193,10 @@
     put(steps - 1, parity, first)
     own_copy = pltpu.make_async_copy(factor_ref.at[own], own_out, own_sem)
     own_copy.start()
+    for step in range(steps):
+        for slot in range(2 * (steps - 1 - step) - 1, 2 * (steps - 1 - step) + 1):
+            for block in range(blocks_reached(step, n_row, n_col), n_row):
+                stage[slot, pl.ds(block, 2 * stretch, stride=n_row), :] = jnp.zeros((2 * stretch, LANES), F32)
     other_norms[...] = row_norms(other[:, width:], scale)
     for step in range(steps)[::-1]:
         for pair, half, row_norm in ((parity, mine, mine_norms), (1 - parity, other, other_norms)):

time: 55.6 us -> 55.8 us (level)
  no operation moved by 1% of the time
where the time goes in v6:
time: 55.8 us; the launch traced here: 55.6 us
  Pallas kernels  31.6 us (57%)
  blocking collectives  21.7 us (39%)
  other arithmetic  0.86 us (2%)
  between operations  0.82 us (1%)
  starting transfers between devices  0.65 us (1%)
    all_to_all x1, blocking collectives, shards(): both = lax.all_to_all(both, ('row', 'col'), 0, 0, tiled=True)  21.7 us
    pallas_call x1, Pallas kernels, shards(): pl.pallas_call(functools.partial(rows_kernel, scale, (n_col, n_col, n_row...  15.2 us
    pallas_call x1, Pallas kernels, shards(): pl.pallas_call(functools.partial(column_kernel, scale, n_row, n_col, stre...  8.67 us
    pallas_call x1, Pallas kernels, shards(): pl.pallas_call(functools.partial(update_kernel, scale, n_row, n_col, stre...  7.76 us
  transfers between devices with their start and end apart: 1, of which 0 were waited for; matrix products, arithmetic and copies ran while one was open for 0% of the time, Pallas kernels for 16%

profile of v6, /device:TPU:1, one launch (start us, length us, event | category | flops | bytes accessed | tf_op | source)
XLA Modules:
  0.0 55.6 jit_solution(5140438452108863602)
XLA Ops:
  0.6 0.9 %compare_select_fusion.2 = s32[128,2,1,128]{3,2,1,0:T(1,128)S(1)} fusion(s32[128]{0:T(128)} %param.5, s32[128]{0:T(128)} %bitcast.9), kind=kLoop, calls=%fused_computation.2 | loop fusion | flops 1048576 | bytes 132096 | tf_op jit(solution)/shard_map/jit(_where)/select_n | solution.py:227
  1.5 21.7 %all_to_all.5.panel_ids = s32[128,2,1,128]{3,2,1,0:T(1,128)S(1)} all-to-all(s32[128,2,1,128]{3,2,1,0:T(1,128)S(1)} %compare_select_fusion.2), channel_id=1, replica_groups=mesh['row'=8,'col'=16] {'row','col'}, dimensions={0} | all-to-all | bytes 262144 | tf_op jit(solution)/shard_map/all_to_all | solution.py:228
  23.2 15.2 %rows.1 = (bf16[1024,2304]{1,0:T(8,128)(2,1)S(1)}, bf16[2048,256]{1,0:T(8,128)(2,1)S(1)}, f32[8,2048]{1,0:T(8,128)S(1)}, bf16[1024,256]{1,0:T(8,128)(2,1)S(1)}, ...) custom-call(bf16[16384,256]{1,0:T(8,128)(2,1)} %teacher.1, bf16[2048,2048]{1,0:T(8,128)(2,1)} %inverse.1, ...), custom_call_target="tpu_custom_call" | custom-call | tf_op jit(solution)/shard_map/rows/pallas_call | solution.py:231
  38.4 0.7 %collective-permute-start = (bf16[1024,2304]{1,0:T(8,128)(2,1)S(1)}, bf16[1024,2304]{1,0:T(8,128)(2,1)S(1)}, u32[]{:S(2)}, u32[]{:S(2)}) collective-permute-start(bf16[1024,2304]{1,0:T(8,128)(2,1)S(1)} %get-tuple-element.13.mine), channel_id=1, source_target_pairs={{0,1},{1,0},{2,3},{3,2},{4,5},{5,4},{6,7},{7,6},{8,9},{9,8},{10,11... | collective-permute-start | bytes 14155784 | tf_op jit(solution)/shard_map/ppermute | solution.py:260
  39.0 8.7 %columns.1 = (bf16[1024,2048]{1,0:T(8,128)(2,1)S(1)}, f32[8,1024]{1,0:T(8,128)S(1)}, f32[2048,128]{1,0:T(8,128)S(1)}) custom-call(bf16[1024,256]{1,0:T(8,128)(2,1)S(1)} %get-tuple-element.14.col_ref, bf16[2048,256]{1,0:T(8,128)(2,1)S(1)} %get-tuple-element.15.panel_ref, f32[8,2048]{1,0:T(8,128)S(1)} %get-tuple-element.16.norm_ref, ...), custom_call_target="tpu_custom_call" | custom-call | flops 8589934592 | bytes 16777216 | tf_op jit(solution)/shard_map/columns/pallas_call | solution.py:263
  47.7 0.0 collective-permute-done.other
  47.7 7.8 %update.1 = (f32[16384,128]{1,0:T(8,128)}, bf16[128,2048]{1,0:T(8,128)(2,1)}) custom-call(bf16[1024,2304]{1,0:T(8,128)(2,1)S(1)} %get-tuple-element.13.mine, bf16[1024,2304]{1,0:T(8,128)(2,1)S(1)} %collective-permute-done.other, bf16[1024,2048]{1,0:T(8,128)(2,1)S(1)} %get-tuple-element.19.factor_ref, bf16[1024,256]{1,0:T(8,128)(2,1)S(1)} %get-tuple-element.14.col_ref, ...), custom_call_target="tpu_custom_call" | custom-call | tf_op jit(solution)/shard_map/update/pallas_call | solution.py:282
Async XLA Ops:
  38.4 9.3 %collective-permute-start = (bf16[1024,2304]{1,0:T(8,128)(2,1)S(1)}, bf16[1024,2304]{1,0:T(8,128)(2,1)S(1)}, u32[]{:S(2)}, u32[]{:S(2)}) collective-permute-start(bf16[1024,2304]{1,0:T(8,128)(2,1)S(1)} %get-tuple-element.13.mine), channel_id=1, source_target_pairs={{0,1},{1,0},{2,3},{3,2},{4,5},{5,4},{6,7},{7,6},{8,9},{9,8},{10,11... | collective-permute-start | bytes 14155784 | tf_op jit(solution)/shard_map/ppermute | solution.py:260
